TPU v7x, 256 devices: a whole 4x4x8 slice. The times are simulated.
256 devices in a mesh: dp: 32 (over z, y), tensor: 8 (over x, core).
Axes of the slice: x: 4, y: 4, z: 8, core: 2. Of those that a mesh axis runs over, the one named last changes fastest.
Arguments:
- cont_q: bfloat16 [640, 64, 8192], P('dp', None, 'tensor'), may hold values from -6 to 6
- cont_k: bfloat16 [640, 64, 1024], P('dp', None, 'tensor'), may hold values from -6 to 6
- cont_v: bfloat16 [640, 64, 1024], P('dp', None, 'tensor'), may hold values from -6 to 6
- out_grad: bfloat16 [640, 64, 8192], P('dp', None, 'tensor'), may hold values from -6 to 6
- prompt_k: bfloat16 [160, 128, 1024], P('dp', 'tensor'), may hold values from -6 to 6
- prompt_v: bfloat16 [160, 128, 1024], P('dp', 'tensor'), may hold values from -6 to 6
- cont_len: int32 [640], P('dp'), may hold values from 16 to 64, as said below
- cont_prompt: int32 [640], replicated, may hold values from 0 to 159, as said below
Outputs:
- attn_out: bfloat16 [640, 64, 8192], P('dp', None, 'tensor')
- grad_q: bfloat16 [640, 64, 8192], P('dp', None, 'tensor')
- grad_k: bfloat16 [640, 64, 1024], P('dp', None, 'tensor')
- grad_v: bfloat16 [640, 64, 1024], P('dp', None, 'tensor')
- grad_prompt_k: float32 [160, 128, 1024], P('dp', 'tensor')
- grad_prompt_v: float32 [160, 128, 1024], P('dp', 'tensor')
Inputs may be any that keep to these rules, and one draw needn't show every extreme that they name: `cont_len`: each index of dp holds some slot of length 64. `cont_prompt`: prompt p is owned by index p // 5 of dp. Each prompt is continued by exactly 4 slots, on 4 different indices of dp. The slots of one index of dp name at most 1 different prompts of any one owner, and some index reaches 1.
All inputs are finite; a program needn't handle non-finite values.
Results may differ from a plain program's by a relative error of at most 0.012.
Values may be sent and summed in bfloat16 or wider, within the bound.
A program may use at most 128 MiB of HBM per device.

v0:
```python
import math

import jax
import jax.numpy as jnp
from jax import lax
from jax.sharding import PartitionSpec as P

HD = 128


def attend(queries, all_keys, all_values, grad_heads, valid_rows):
    score_scale = 1.0 / math.sqrt(queries.shape[-1])
    seq_len = queries.shape[1]
    key_count = all_keys.shape[1]
    prefix_len = key_count - seq_len
    scores = (
        jnp.einsum("slhgd,skhd->shglk", queries, all_keys, preferred_element_type=jnp.float32)
        * score_scale
    )
    row_index = lax.broadcasted_iota(jnp.int32, (seq_len, key_count), 0)
    col_index = lax.broadcasted_iota(jnp.int32, (seq_len, key_count), 1)
    scores = jnp.where(col_index <= row_index + prefix_len, scores, -jnp.inf)
    row_max = jnp.max(scores, axis=-1, keepdims=True)
    exponent = jnp.exp(scores - row_max)
    probability = exponent / jnp.sum(exponent, axis=-1, keepdims=True)
    weights = probability.astype(jnp.bfloat16)
    row_valid = valid_rows[:, :, None, None, None]
    attended = jnp.einsum(
        "shglk,skhd->slhgd", weights, all_values, preferred_element_type=jnp.float32
    )
    attended = (attended * row_valid.astype(jnp.float32)).astype(jnp.bfloat16)
    masked = grad_heads * row_valid.astype(jnp.bfloat16)
    dweights = jnp.einsum(
        "slhgd,skhd->shglk", masked, all_values, preferred_element_type=jnp.float32
    )
    row_delta = jnp.sum(probability * dweights, axis=-1, keepdims=True)
    dscores = (probability * (dweights - row_delta) * score_scale).astype(jnp.bfloat16)
    dquery = jnp.einsum(
        "shglk,skhd->slhgd", dscores, all_keys, preferred_element_type=jnp.float32
    ).astype(jnp.bfloat16)
    dkey = jnp.einsum("shglk,slhgd->skhd", dscores, queries, preferred_element_type=jnp.float32)
    dvalue = jnp.einsum("shglk,slhgd->skhd", weights, masked, preferred_element_type=jnp.float32)
    return (attended, dquery, dkey, dvalue)


def on_device(cont_q, cont_k, cont_v, out_grad, prompt_k, prompt_v, cont_len, cont_prompt):
    head_k, head_v = (
        lax.all_to_all(prompt_k, "tensor", split_axis=2, concat_axis=1, tiled=True),
        lax.all_to_all(prompt_v, "tensor", split_axis=2, concat_axis=1, tiled=True),
    )
    slot_count, seq_len, q_width = cont_q.shape
    kv_width = cont_k.shape[2]
    kv_local = kv_width // HD
    group_size = q_width // kv_width
    dp_count = lax.axis_size("dp")
    my_index = lax.axis_index("dp")
    local_prompts = head_k.shape[0]
    prefix_len = head_k.shape[1]
    prompt_total = dp_count * local_prompts
    my_prompts = lax.dynamic_slice_in_dim(cont_prompt, my_index * slot_count, slot_count)
    all_prompt_k, all_prompt_v = (
        lax.all_gather(head_k, "dp", axis=0, tiled=True),
        lax.all_gather(head_v, "dp", axis=0, tiled=True),
    )
    pre_k = jnp.take(all_prompt_k, my_prompts, axis=0)
    pre_v = jnp.take(all_prompt_v, my_prompts, axis=0)
    key_count = prefix_len + seq_len
    valid_rows = lax.broadcasted_iota(jnp.int32, (slot_count, seq_len), 1) < cont_len[:, None]
    queries = cont_q.reshape(slot_count, seq_len, kv_local, group_size, HD)
    all_keys = jnp.concatenate((pre_k, cont_k), axis=1).reshape(slot_count, key_count, kv_local, HD)
    all_values = jnp.concatenate((pre_v, cont_v), axis=1).reshape(
        slot_count, key_count, kv_local, HD
    )
    grad_heads = out_grad.reshape(slot_count, seq_len, kv_local, group_size, HD)
    attended, dquery, dkey, dvalue = attend(queries, all_keys, all_values, grad_heads, valid_rows)
    attn_out = attended.reshape(slot_count, seq_len, q_width)
    grad_q = dquery.reshape(slot_count, seq_len, q_width)
    grad_k = dkey[:, prefix_len:].reshape(slot_count, seq_len, kv_width).astype(jnp.bfloat16)
    grad_v = dvalue[:, prefix_len:].reshape(slot_count, seq_len, kv_width).astype(jnp.bfloat16)
    pre_dk = dkey[:, :prefix_len].reshape(slot_count, prefix_len, kv_width)
    pre_dv = dvalue[:, :prefix_len].reshape(slot_count, prefix_len, kv_width)
    prompt_onehot = (
        my_prompts[:, None] == lax.broadcasted_iota(jnp.int32, (1, prompt_total), 1)
    ).astype(jnp.float32)
    table_k = jnp.einsum("sp,sxc->pxc", prompt_onehot, pre_dk, precision=lax.Precision.HIGHEST)
    table_v = jnp.einsum("sp,sxc->pxc", prompt_onehot, pre_dv, precision=lax.Precision.HIGHEST)
    owned_k, owned_v = (
        lax.psum_scatter(
            table_k.astype(jnp.bfloat16), "dp", scatter_dimension=0, tiled=True
        ).astype(jnp.float32),
        lax.psum_scatter(
            table_v.astype(jnp.bfloat16), "dp", scatter_dimension=0, tiled=True
        ).astype(jnp.float32),
    )
    grad_prompt_k, grad_prompt_v = (
        lax.all_to_all(
            owned_k.astype(jnp.bfloat16), "tensor", split_axis=1, concat_axis=2, tiled=True
        ).astype(owned_k.dtype),
        lax.all_to_all(
            owned_v.astype(jnp.bfloat16), "tensor", split_axis=1, concat_axis=2, tiled=True
        ).astype(owned_v.dtype),
    )
    return (attn_out, grad_q, grad_k, grad_v, grad_prompt_k, grad_prompt_v)


def solution(mesh):
    return jax.shard_map(
        on_device,
        mesh=mesh,
        in_specs=(
            P("dp", None, "tensor"),
            P("dp", None, "tensor"),
            P("dp", None, "tensor"),
            P("dp", None, "tensor"),
            P("dp", "tensor", None),
            P("dp", "tensor", None),
            P("dp"),
            P(),
        ),
        out_specs=(
            P("dp", None, "tensor"),
            P("dp", None, "tensor"),
            P("dp", None, "tensor"),
            P("dp", None, "tensor"),
            P("dp", "tensor", None),
            P("dp", "tensor", None),
        ),
        check_vma=False,
    )
```

profile of v0, /device:TPU:1, one launch (start us, length us, event | category | flops | bytes accessed | tf_op | source)
XLA Modules:
  0.0 712.6 jit_solution(10385616208360097809)
XLA Ops:
  7.2 3.4 copy.61
  10.7 2.5 reshape.184
  13.2 11.2 %all_to_all.54 = bf16[8,2,5120]{2,1,0:T(2,128)(2,1)S(1)} all-to-all(bf16[8,2,5120]{2,1,0:T(2,128)(2,1)S(1)} %reshape.184), channel_id=1, replica_groups=mesh['dp'=32,'tensor'=8] {'tensor'}, dimensions={0} | all-to-all | bytes 327680 | tf_op jit(solution)/shard_map/all_to_all | solution.py:48
  26.7 2.8 copy.63
  29.6 2.4 copy.58
  32.0 2.5 reshape.182
  34.6 8.9 %all_to_all.55 = bf16[8,2,5120]{2,1,0:T(2,128)(2,1)S(1)} all-to-all(bf16[8,2,5120]{2,1,0:T(2,128)(2,1)S(1)} %reshape.182), channel_id=1, replica_groups=mesh['dp'=32,'tensor'=8] {'tensor'}, dimensions={0} | all-to-all | bytes 327680 | tf_op jit(solution)/shard_map/all_to_all | solution.py:49
  45.7 2.8 copy.60
  49.7 64.1 %all-gather.5.cloned.1.call-done = bf16[160,128,128]{2,1,0:T(8,128)(2,1)} async-done(((bf16[5,128,128]{2,1,0:T(8,128)(2,1)}), bf16[160,128,128]{2,1,0:T(8,128)(2,1)}) %all-gather.5.cloned.1.call-update) | async-done | bytes 5242896 | tf_op jit(solution)/shard_map/all_gather | solution.py:62
  113.8 4.0 gather_fusion.1
  117.8 81.5 %all-gather.3.cloned.1.call-done = bf16[160,128,128]{2,1,0:T(8,128)(2,1)} async-done(((bf16[5,128,128]{2,1,0:T(8,128)(2,1)}), bf16[160,128,128]{2,1,0:T(8,128)(2,1)}) %all-gather.3.cloned.1.call-update) | async-done | bytes 5242896 | tf_op jit(solution)/shard_map/all_gather | solution.py:63
  199.3 4.0 gather_fusion
  204.8 3.2 fusion.6
  208.0 3.6 fusion.5
  212.0 8.5 %fusion = (f32[20,8,64]{2,1,0:T(8,128)S(1)}, f32[20,192,64,8]{1,2,3,0:T(8,128)}) fusion(f32[20,8,64]{2,1,0:T(8,128)S(1)} %fusion.5, f32[20,8,64]{2,1,0:T(8,128)S(1)} %get-tuple-element.13, f32[20,192,64,8]{1,2,3,0:T(8,128)S(1)} %get-tuple-element.14, pred[64,192]{1,0:T(8,128)(4,1)S(1)} %iota_compare_fusion, bf16[20,64]{1,0:T(8,128)(2,1)S(1)} %get-tuple-element.9, ...), kind=kOutput, calls=%fused_computation.5 | convolution fusion | flops 522311680 | bytes 19470848 | tf_op jit(solution)/shard_map/slhgd,skhd->shglk/dot_general | solution.py:33
  220.4 6.3 fusion.7
  229.3 5.1 convolution_convert_fusion.1
  234.4 4.3 copy.70
  240.4 11.1 %fusion.27 = f32[20,192,1,128]{3,1,0,2:T(8,128)S(1)} fusion(bf16[20,64]{1,0:T(8,128)(2,1)S(1)} %get-tuple-element.9, f32[20,8,64]{2,1,0:T(8,128)S(1)} %fusion.5, f32[20,8,64]{2,1,0:T(8,128)S(1)} %get-tuple-element.13, f32[20,192,64,8]{1,2,3,0:T(8,128)} %copy-done.2, pred[64,192]{1,0:T(8,128)(4,1)S(1)} %iota_compare_fusion, ...), kind=kOutput, calls=%fused_computation.34 | convolution fusion | flops 518389760 | bytes 12548608 | tf_op jit(solution)/shard_map/shglk,slhgd->skhd/dot_general | solution.py:42
  253.0 5.1 convolution_convert_fusion
  258.1 4.4 copy.74
  263.7 6.4 fusion.14
  270.1 2.3 copy.65
  272.4 3.1 reshape.145
  275.5 4.2 convert_bitcast_fusion
  279.7 3.9 copy.67
  283.6 5.2 reshape.148
  288.8 170.5 %reduce-scatter.3.cloned.1.call-done = bf16[5,128,128]{2,1,0:T(8,128)(2,1)} async-done(((bf16[160,128,128]{2,1,0:T(8,128)(2,1)}), bf16[5,128,128]{2,1,0:T(8,128)(2,1)}) %reduce-scatter.3.cloned.1.call-update) | async-done | bytes 163856 | tf_op jit(solution)/shard_map/reduce_scatter | solution.py:88
  461.0 9.7 %all-to-all-start.2 = ((bf16[5,128,128]{2,0,1:T(8,128)(2,1)}), bf16[5,128,128]{2,0,1:T(8,128)(2,1)S(1)}, u32[]{:S(2)}, u32[]{:S(2)}) async-start(bf16[5,128,128]{2,0,1:T(8,128)(2,1)} %copy.71), calls=%async_computation.3 | async-start | bytes 524288 | tf_op jit(solution)/shard_map/all_to_all | solution.py:96
  472.9 214.1 %reduce-scatter.5.cloned.1.call-done = bf16[5,128,128]{2,1,0:T(8,128)(2,1)} async-done(((bf16[160,128,128]{2,1,0:T(8,128)(2,1)}), bf16[5,128,128]{2,1,0:T(8,128)(2,1)}) %reduce-scatter.5.cloned.1.call-update) | async-done | bytes 163856 | tf_op jit(solution)/shard_map/reduce_scatter | solution.py:91
  688.8 9.7 %all-to-all-start.3 = ((bf16[5,128,128]{2,0,1:T(8,128)(2,1)}), bf16[5,128,128]{2,0,1:T(8,128)(2,1)S(1)}, u32[]{:S(2)}, u32[]{:S(2)}) async-start(bf16[5,128,128]{2,0,1:T(8,128)(2,1)} %copy.75), calls=%async_computation.5 | async-start | bytes 524288 | tf_op jit(solution)/shard_map/all_to_all | solution.py:99
  699.5 5.5 all-to-all-done.3
  (58 shorter events, 22.2 us)
Async XLA Ops:
  7.2 197.6 %copy-start = (bf16[20,64,1024]{2,1,0:T(8,128)(2,1)S(1)}, bf16[20,64,1024]{2,1,0:T(8,128)(2,1)}, u32[]{:S(2)}) copy-start(bf16[20,64,1024]{2,1,0:T(8,128)(2,1)} %param.10) | copy-start | bytes 7864324
  7.2 22.4 %copy-start.8 = (bf16[5,16,1024]{2,1,0:T(8,128)(2,1)S(1)}, bf16[5,16,1024]{2,1,0:T(8,128)(2,1)}, u32[]{:S(2)}) copy-start(bf16[5,16,1024]{2,1,0:T(8,128)(2,1)} %param.15) | copy-start | bytes 491524
  7.2 106.6 %all-gather.5.cloned.1.call-start = ((), (), s32[]{:S(2)}) async-start(), calls=%async_computation.7 | async-start | bytes 5406720 | tf_op jit(solution)/shard_map/all_gather | solution.py:62
  29.5 20.1 %copy-start.9 = (s32[20]{0:T(128)S(1)}, s32[20]{0:T(128)}, u32[]{:S(2)}) copy-start(s32[20]{0:T(128)} %param.16) | copy-start | bytes 244
  29.5 169.8 %all-gather.3.cloned.1.call-start = ((), (), s32[]{:S(2)}) async-start(), calls=%async_computation.6 | async-start | bytes 5406720 | tf_op jit(solution)/shard_map/all_gather | solution.py:63
  48.5 410.7 %reduce-scatter.3.cloned.1.call-start = ((), (), s32[]{:S(2)}) async-start(), calls=%async_computation.8 | async-start | bytes 5406720 | tf_op jit(solution)/shard_map/reduce_scatter | solution.py:88
  204.8 6.9 copy-start.6
  208.0 12.5 %copy-start.2 = (f32[20,192,64,8]{1,2,3,0:T(8,128)}, f32[20,192,64,8]{1,2,3,0:T(8,128)S(1)}, u32[]{:S(2)}) copy-start(f32[20,192,64,8]{1,2,3,0:T(8,128)S(1)} %get-tuple-element.14) | copy-start | bytes 23592964
  208.0 3.7 copy-start.10
  208.0 4.0 copy-start.12
  226.8 2.3 copy-start.3
  229.1 5.2 copy-start.4
  238.6 1.7 copy-start.11
  238.7 448.4 %reduce-scatter.5.cloned.1.call-start = ((), (), s32[]{:S(2)}) async-start(), calls=%async_computation.9 | async-start | bytes 5406720 | tf_op jit(solution)/shard_map/reduce_scatter | solution.py:91
  251.5 1.4 copy-start.5
  262.5 1.1 copy-start.7
  262.5 1.2 copy-start.13
  279.7 426.4 %copy-start.1 = (bf16[20,64,1024]{2,1,0:T(8,128)(2,1)S(1)}, bf16[20,64,1024]{2,1,0:T(8,128)(2,1)}, u32[]{:S(2)}) copy-start(bf16[20,64,1024]{2,1,0:T(8,128)(2,1)} %param.10) | copy-start | bytes 7864324
  461.0 227.8 %all-to-all-start.2 = ((bf16[5,128,128]{2,0,1:T(8,128)(2,1)}), bf16[5,128,128]{2,0,1:T(8,128)(2,1)S(1)}, u32[]{:S(2)}, u32[]{:S(2)}) async-start(bf16[5,128,128]{2,0,1:T(8,128)(2,1)} %copy.71), calls=%async_computation.3 | async-start | bytes 524288 | tf_op jit(solution)/shard_map/all_to_all | solution.py:96
  688.8 16.3 %all-to-all-start.3 = ((bf16[5,128,128]{2,0,1:T(8,128)(2,1)}), bf16[5,128,128]{2,0,1:T(8,128)(2,1)S(1)}, u32[]{:S(2)}, u32[]{:S(2)}) async-start(bf16[5,128,128]{2,0,1:T(8,128)(2,1)} %copy.75), calls=%async_computation.5 | async-start | bytes 524288 | tf_op jit(solution)/shard_map/all_to_all | solution.py:99
Sparse Core Ops, SparseCore 0:
  29.6 84.1 all-gather.4
  117.0 82.2 all-gather.2
  238.8 220.3 reduce-scatter.2
  463.0 223.9 reduce-scatter.4
where the time goes:
time: 714 us; the launch traced here: 713 us
  waiting for transfers between devices  536 us (75%)
  local copies, waits for them, and re-layouts  65.1 us (9%)
  matrix products  45.1 us (6%)
  starting transfers between devices  20.1 us (3%)
  blocking collectives  20.1 us (3%)
  between operations  14.1 us (2%)
  other arithmetic  12.4 us (2%)
    reduce_scatter x1, waiting for transfers between devices, on_device(): lax.psum_scatter(table_v.astype(jnp.bfloat16), 'dp', scatter_dimension=0,...  214 us
    reduce_scatter x1, waiting for transfers between devices, on_device(): lax.psum_scatter(table_k.astype(jnp.bfloat16), 'dp', scatter_dimension=0,...  170 us
    all_gather x1, waiting for transfers between devices, on_device(): lax.all_gather(head_v, 'dp', axis=0, tiled=True)  81.5 us
    all_gather x1, waiting for transfers between devices, on_device(): lax.all_gather(head_k, 'dp', axis=0, tiled=True)  64.1 us
    unnamed x34, local copies, waits for them, and re-layouts  20.6 us
  transfers between devices with their start and end apart: 6, of which 5 were waited for; matrix products, arithmetic and copies ran while one was open for 9% of the time, Pallas kernels for 0%

commit v1 on v0

v1 whole, which is shorter than its diff:
```python
import functools
import math

import jax
import jax.numpy as jnp
from jax import lax
from jax.experimental import pallas as pl
from jax.experimental.pallas import tpu as pltpu
from jax.sharding import PartitionSpec as P

HD = 128
NY = 4
NEG = -1e30
MESH = pl.DeviceIdType.MESH
BF16 = jnp.bfloat16
F32 = jnp.float32


def coordinates(n_dp, n_t):
    dp = lax.axis_index("dp")
    t = lax.axis_index("tensor")
    z, y = dp // NY, dp % NY
    nz = n_dp // NY

    def at_z(step):
        return (lax.rem(z + step + nz, nz) * NY + y, t)

    def at_y(step):
        return (z * NY + lax.rem(y + step + NY, NY), t)

    def at_t(step):
        return (dp, lax.rem(t + step + n_t, n_t))

    return z, y, t, at_z, at_y, at_t


def greet(partners):
    barrier = pltpu.get_barrier_semaphore()
    for partner in partners:
        pl.semaphore_signal(barrier, inc=1, device_id=partner, device_id_type=MESH)
    pl.semaphore_wait(barrier, len(partners))


def remote(src, dst, send, recv, device):
    return pltpu.make_async_remote_copy(
        src_ref=src,
        dst_ref=dst,
        send_sem=send,
        recv_sem=recv,
        device_id=device,
        device_id_type=MESH,
    )


def ring_partners(nz, n_t, at_z, at_y, at_t):
    return (
        [at_t(j) for j in range(1, n_t)]
        + [at_z(1), at_z(-1)]
        + [at_y(u) for u in range(1, NY)]
    )


def gather_kernel(n_dp, n_t, m_ref, pk_ref, pv_ref, out_ref, *scratch):
    nz = n_dp // NY
    half = nz // 2
    blocks = [list(scratch[:nz]), list(scratch[nz : 2 * nz])]
    ysend, relay = scratch[2 * nz : 2 * nz + 2]
    xs, xr, xl, zs, zr, ys, yr, yl, rs, rr = scratch[2 * nz + 2 :]
    z, y, t, at_z, at_y, at_t = coordinates(n_dp, n_t)
    share = pk_ref.shape[1]
    greet(ring_partners(nz, n_t, at_z, at_y, at_t))
    sent = []

    for kv, ref in enumerate((pk_ref, pv_ref)):
        mine = pl.ds(pl.multiple_of(t * share, share), share)
        for j in range(1, n_t):
            to = at_t(j)
            cols = pl.ds(pl.multiple_of(to[1] * HD, HD), HD)
            copy = remote(
                ref.at[:, :, cols], blocks[kv][0].at[:, mine, :], xs.at[kv, j], xr.at[kv, j], to
            )
            copy.start()
            sent.append(copy)
        cols = pl.ds(pl.multiple_of(t * HD, HD), HD)
        pltpu.make_async_copy(
            ref.at[:, :, cols], blocks[kv][0].at[:, mine, :], xl.at[kv]
        ).start()

    def wait_own(kv):
        mine = pl.ds(pl.multiple_of(t * share, share), share)
        cols = pl.ds(pl.multiple_of(t * HD, HD), HD)
        ref = (pk_ref, pv_ref)[kv]
        pltpu.make_async_copy(
            ref.at[:, :, cols], blocks[kv][0].at[:, mine, :], xl.at[kv]
        ).wait()
        for j in range(1, n_t):
            src_t = lax.rem(t - j + n_t, n_t)
            rows = pl.ds(pl.multiple_of(src_t * share, share), share)
            remote(
                ref.at[:, :, cols], blocks[kv][0].at[:, rows, :], xs.at[kv, j], xr.at[kv, j], at_t(j)
            ).wait_recv()

    def push(kv, r, direction):
        nxt = (r + direction) % nz
        copy = remote(
            blocks[kv][r], blocks[kv][nxt], zs.at[kv, nxt], zr.at[kv, nxt], at_z(direction)
        )
        copy.start()
        sent.append(copy)

    def wait_block(kv, r):
        remote(
            blocks[kv][r], blocks[kv][r], zs.at[kv, r], zr.at[kv, r], at_z(1)
        ).wait_recv()

    local = []

    def spread(r):
        row = lax.rem(z - r + nz, nz)
        for u in (2, 1, 3, 0):
            to = at_y(u)
            pick = jnp.maximum(m_ref[to[0], row * NY + y], 0)
            for kv in range(2):
                ysend[r, u, kv] = blocks[kv][r][pick]
            if u == 0:
                copy = pltpu.make_async_copy(ysend.at[r, 0], out_ref.at[r * NY], yl.at[r])
                copy.start()
                local.append(copy)
            elif u == 2:
                for kv, way in enumerate((1, -1)):
                    copy = remote(
                        ysend.at[r, u, kv], relay.at[r, kv], rs.at[r, kv], rr.at[r, kv], at_y(way)
                    )
                    copy.start()
                    sent.append(copy)
            else:
                copy = remote(
                    ysend.at[r, u], out_ref.at[r * NY + u], ys.at[r, u], yr.at[r, u], to
                )
                copy.start()
                sent.append(copy)

    def forward(r):
        for kv, way in enumerate((1, -1)):
            remote(
                ysend.at[r, 2, kv], relay.at[r, kv], rs.at[r, kv], rr.at[r, kv], at_y(way)
            ).wait_recv()
            slot = 2 if kv == 0 else 0
            copy = remote(
                relay.at[r, kv], out_ref.at[r * NY + 2, kv], ys.at[r, slot], yr.at[r, slot], at_y(way)
            )
            copy.start()
            sent.append(copy)

    for kv in range(2):
        wait_own(kv)
        push(kv, 0, 1)
        push(kv, 0, -1)
    spread(0)
    waiting = [0]
    for h in range(1, half + 1):
        for kv in range(2):
            right_hops = half if kv == 0 else half - 1
            left_hops = nz - 1 - right_hops
            if h <= right_hops:
                wait_block(kv, h)
                if h < right_hops:
                    push(kv, h, 1)
            if h <= left_hops:
                wait_block(kv, nz - h)
                if h < left_hops:
                    push(kv, nz - h, -1)
        todo, waiting = waiting, [h] if h == half else [h, nz - h]
        for r in waiting:
            spread(r)
        for r in todo:
            forward(r)
    for r in waiting:
        forward(r)
    for copy in sent:
        copy.wait_send()
    for copy in local:
        copy.wait()
    for r in range(nz):
        for u in (1, 3):
            remote(
                ysend.at[r, u], out_ref.at[r * NY + u], ys.at[r, u], yr.at[r, u], at_y(u)
            ).wait_recv()
        for kv, slot in ((0, 2), (1, 0)):
            remote(
                relay.at[r, kv], out_ref.at[r * NY + 2, kv], ys.at[r, slot], yr.at[r, slot], at_y(1)
            ).wait_recv()


def gather_prompts(n_dp, n_t, table, pk, pv):
    nz = n_dp // NY
    per, share, width = pk.shape
    plen = share * n_t
    dma = pltpu.SemaphoreType.DMA
    return pl.pallas_call(
        functools.partial(gather_kernel, n_dp, n_t),
        out_shape=jax.ShapeDtypeStruct((n_dp, 2, plen, HD), BF16),
        in_specs=[
            pl.BlockSpec(memory_space=pltpu.SMEM),
            pl.BlockSpec(memory_space=pl.ANY),
            pl.BlockSpec(memory_space=pl.ANY),
        ],
        out_specs=pl.BlockSpec(memory_space=pl.ANY),
        scratch_shapes=[pltpu.VMEM((per, plen, HD), BF16) for _ in range(2 * nz)]
        + [
            pltpu.VMEM((nz, NY, 2, plen, HD), BF16),
            pltpu.VMEM((nz, 2, plen, HD), BF16),
            dma((2, n_t)),
            dma((2, n_t)),
            dma((2,)),
            dma((2, nz)),
            dma((2, nz)),
            dma((nz, NY)),
            dma((nz, NY)),
            dma((nz,)),
            dma((nz, 2)),
            dma((nz, 2)),
        ],
        compiler_params=pltpu.CompilerParams(
            collective_id=0, has_side_effects=True, vmem_limit_bytes=32 * 2**20
        ),
        name="gather_prompts",
    )(table, pk, pv)


def scatter_kernel(n_dp, n_t, m_ref, g_ref, ok_ref, ov_ref, *scratch):
    nz = n_dp // NY
    half = nz // 2
    arrived, relay, total, pieces = scratch[:4]
    chain = [[list(scratch[4 + (d * 2 + kv) * nz : 4 + (d * 2 + kv + 1) * nz]) for kv in range(2)] for d in range(2)]
    ys, yr, yl, rs, rr, zs, zr, xs, xr = scratch[4 + 4 * nz :]
    z, y, t, at_z, at_y, at_t = coordinates(n_dp, n_t)
    per, share = ok_ref.shape[:2]
    greet(ring_partners(nz, n_t, at_z, at_y, at_t))
    sent = []
    order = [half]
    for h in range(1, half):
        order += [half + h, half - h]
    order.append(0)

    def send_out(r):
        for u in (2, 1, 3):
            if u == 2:
                for kv, way in enumerate((-1, 1)):
                    copy = remote(
                        g_ref.at[r * NY + 2, kv], relay.at[r, kv], rs.at[r, kv], rr.at[r, kv], at_y(way)
                    )
                    copy.start()
                    sent.append(copy)
            else:
                copy = remote(
                    g_ref.at[r * NY + u], arrived.at[r, u], ys.at[r, u], yr.at[r, u], at_y(-u)
                )
                copy.start()
                sent.append(copy)
        pltpu.make_async_copy(g_ref.at[r * NY], arrived.at[r, 0], yl.at[r]).start()

    def forward(r):
        for kv, way in enumerate((-1, 1)):
            remote(
                g_ref.at[r * NY + 2, kv], relay.at[r, kv], rs.at[r, kv], rr.at[r, kv], at_y(way)
            ).wait_recv()
            slot = 2 if kv == 0 else 0
            copy = remote(
                relay.at[r, kv], arrived.at[r, 2, kv], ys.at[r, slot], yr.at[r, slot], at_y(way)
            )
            copy.start()
            sent.append(copy)

    def wait_y(r):
        pltpu.make_async_copy(g_ref.at[r * NY], arrived.at[r, 0], yl.at[r]).wait()
        for u in (1, 3):
            remote(
                g_ref.at[r * NY + u], arrived.at[r, u], ys.at[r, u], yr.at[r, u], at_y(-u)
            ).wait_recv()
        for kv, slot in ((0, 2), (1, 0)):
            remote(
                relay.at[r, kv], arrived.at[r, 2, kv], ys.at[r, slot], yr.at[r, slot], at_y(1)
            ).wait_recv()

    def term(r, kv, p):
        row = lax.rem(z - r + nz, nz)
        acc = None
        for u in range(NY):
            which = m_ref[at_y(u)[0], row * NY + y]
            piece = jnp.where(which == p, arrived[r, u, kv].astype(F32), 0.0)
            acc = piece if acc is None else acc + piece
        return acc

    def wait_chain(d, kv, r):
        remote(
            chain[d][kv][r], chain[d][kv][r], zs.at[d, kv, r], zr.at[d, kv, r], at_z(1)
        ).wait_recv()

    def pass_on(d, kv, r):
        step = 1 if d == 0 else -1
        nxt = (r + step) % nz
        copy = remote(
            chain[d][kv][r], chain[d][kv][nxt], zs.at[d, kv, nxt], zr.at[d, kv, nxt], at_z(step)
        )
        copy.start()
        sent.append(copy)

    def reduce_block(r):
        d = 0 if r >= half else 1
        for kv in range(2):
            way = d if r != half else kv
            first = r == half if kv == way else r == (half + 1 if way == 0 else half - 1)
            buf = chain[way][kv][r]
            if not first:
                wait_chain(way, kv, r)
            for p in range(per):
                value = term(r, kv, p)
                if not first:
                    value = value + buf[p].astype(F32)
                buf[p] = value.astype(BF16)
            pass_on(way, kv, r)

    for r in order:
        send_out(r)
    forward(order[0])
    for h in range(1, half):
        forward(half + h)
        forward(half - h)
        for r in [half] if h == 1 else [half + h - 1, half - h + 1]:
            wait_y(r)
            reduce_block(r)
    forward(0)
    for r in (nz - 1, 1):
        wait_y(r)
        reduce_block(r)
    wait_y(0)
    for kv in range(2):
        for d in range(2):
            wait_chain(d, kv, 0)
        for p in range(per):
            value = term(0, kv, p) + chain[0][kv][0][p].astype(F32) + chain[1][kv][0][p].astype(F32)
            total[kv, p] = value.astype(BF16)
        for j in range(1, n_t):
            to = at_t(j)
            rows = pl.ds(pl.multiple_of(to[1] * share, share), share)
            copy = remote(
                total.at[kv, :, rows, :], pieces.at[kv, j], xs.at[kv, j], xr.at[kv, j], to
            )
            copy.start()
            sent.append(copy)
        rows = pl.ds(pl.multiple_of(t * share, share), share)
        cols = pl.ds(pl.multiple_of(t * HD, HD), HD)
        (ok_ref, ov_ref)[kv][:, :, cols] = total[kv, :, rows, :].astype(F32)
    for kv in range(2):
        for j in range(1, n_t):
            rows = pl.ds(pl.multiple_of(t * share, share), share)
            remote(
                total.at[kv, :, rows, :], pieces.at[kv, j], xs.at[kv, j], xr.at[kv, j], at_t(j)
            ).wait_recv()
            cols = pl.ds(pl.multiple_of(at_t(-j)[1] * HD, HD), HD)
            (ok_ref, ov_ref)[kv][:, :, cols] = pieces[kv, j].astype(F32)
    for copy in sent:
        copy.wait_send()


def scatter_grads(n_dp, n_t, table, grads, per, share):
    nz = n_dp // NY
    plen = share * n_t
    dma = pltpu.SemaphoreType.DMA
    out = jax.ShapeDtypeStruct((per, share, n_t * HD), F32)
    return pl.pallas_call(
        functools.partial(scatter_kernel, n_dp, n_t),
        out_shape=(out, out),
        in_specs=[
            pl.BlockSpec(memory_space=pltpu.SMEM),
            pl.BlockSpec(memory_space=pl.ANY),
        ],
        out_specs=[pl.BlockSpec(memory_space=pltpu.VMEM)] * 2,
        scratch_shapes=[
            pltpu.VMEM((nz, NY, 2, plen, HD), BF16),
            pltpu.VMEM((nz, 2, plen, HD), BF16),
            pltpu.VMEM((2, per, plen, HD), BF16),
            pltpu.VMEM((2, n_t, per, share, HD), BF16),
        ]
        + [pltpu.VMEM((per, plen, HD), BF16) for _ in range(4 * nz)]
        + [
            dma((nz, NY)),
            dma((nz, NY)),
            dma((nz,)),
            dma((nz, 2)),
            dma((nz, 2)),
            dma((2, 2, nz)),
            dma((2, 2, nz)),
            dma((2, n_t)),
            dma((2, n_t)),
        ],
        compiler_params=pltpu.CompilerParams(
            collective_id=1, has_side_effects=True, vmem_limit_bytes=32 * 2**20
        ),
        name="scatter_grads",
    )(table, grads)


def dot(a, b, dims):
    return lax.dot_general(a, b, (dims, ((), ())), preferred_element_type=F32)


def attend_slot(length, queries, cotangent, keys, values, heads):
    rows = queries.shape[0]
    count = keys.shape[0]
    tokens = rows // heads
    prefix = count - tokens
    scale = 1.0 / math.sqrt(HD)
    token = lax.rem(lax.broadcasted_iota(jnp.int32, (1, rows), 1), tokens)
    valid = lax.rem(lax.broadcasted_iota(jnp.int32, (rows, 1), 0), tokens) < length
    cotangent = jnp.where(valid, cotangent, jnp.zeros_like(cotangent))
    scores = dot(keys, queries, ((1,), (1,)))
    dweights = dot(values, cotangent, ((1,), (1,)))
    key = lax.broadcasted_iota(jnp.int32, (tokens, rows), 0)
    tail = jnp.where(key <= token, scores[prefix:], NEG)
    scores = jnp.concatenate([scores[:prefix], tail], axis=0)
    top = jnp.max(scores, axis=0, keepdims=True)
    exponent = jnp.exp2((scores - top) * (scale * math.log2(math.e)))
    probs = exponent * (1.0 / jnp.sum(exponent, axis=0, keepdims=True))
    weights = probs.astype(BF16)
    delta = jnp.sum(probs * dweights, axis=0, keepdims=True)
    dscores = (probs * (dweights - delta) * scale).astype(BF16)
    out = dot(weights, values, ((0,), (0,)))
    out = jnp.where(valid, out, 0.0).astype(BF16)
    dq = dot(dscores, keys, ((0,), (0,))).astype(BF16)
    dk = dot(dscores, queries, ((1,), (0,)))
    dv = dot(weights, cotangent, ((1,), (0,)))
    return out, dq, dk, dv


def attend_kernel(
    batch, index_ref, len_ref, q_ref, do_ref, ck_ref, cv_ref, pre_ref, out_ref, dq_ref, dk_ref, dv_ref, g_ref
):
    step = pl.program_id(0)
    heads = q_ref.shape[2] // HD
    tokens = q_ref.shape[1]
    prefix = pre_ref.shape[2]
    for b in range(batch):
        s = step * batch + b
        place = index_ref[s]
        queries = jnp.concatenate([q_ref[b, :, h * HD : (h + 1) * HD] for h in range(heads)], axis=0)
        cotangent = jnp.concatenate([do_ref[b, :, h * HD : (h + 1) * HD] for h in range(heads)], axis=0)
        keys = jnp.concatenate([pre_ref[place, 0], ck_ref[b]], axis=0)
        values = jnp.concatenate([pre_ref[place, 1], cv_ref[b]], axis=0)
        out, dq, dk, dv = attend_slot(len_ref[s], queries, cotangent, keys, values, heads)
        for h in range(heads):
            out_ref[b, :, h * HD : (h + 1) * HD] = out[h * tokens : (h + 1) * tokens]
            dq_ref[b, :, h * HD : (h + 1) * HD] = dq[h * tokens : (h + 1) * tokens]
        dk_ref[b] = dk[prefix:].astype(BF16)
        dv_ref[b] = dv[prefix:].astype(BF16)
        g_ref[place, 0] = dk[:prefix].astype(BF16)
        g_ref[place, 1] = dv[:prefix].astype(BF16)


def attend(index, cont_len, q, do, ck, cv, pre, batch=2):
    slots, tokens, width = q.shape
    wide = pl.BlockSpec((batch, tokens, width), lambda i, *_: (i, 0, 0))
    thin = pl.BlockSpec((batch, tokens, HD), lambda i, *_: (i, 0, 0))
    whole = pl.BlockSpec(pre.shape, lambda i, *_: (0, 0, 0, 0))
    flops = 12 * slots * tokens * (tokens + pre.shape[2]) * width
    return pl.pallas_call(
        functools.partial(attend_kernel, batch),
        grid_spec=pltpu.PrefetchScalarGridSpec(
            num_scalar_prefetch=2,
            grid=(slots // batch,),
            in_specs=[wide, wide, thin, thin, whole],
            out_specs=[wide, wide, thin, thin, whole],
        ),
        out_shape=(
            jax.ShapeDtypeStruct(q.shape, BF16),
            jax.ShapeDtypeStruct(q.shape, BF16),
            jax.ShapeDtypeStruct(ck.shape, BF16),
            jax.ShapeDtypeStruct(cv.shape, BF16),
            jax.ShapeDtypeStruct(pre.shape, BF16),
        ),
        compiler_params=pltpu.CompilerParams(vmem_limit_bytes=40 * 2**20),
        cost_estimate=pl.CostEstimate(flops=flops, bytes_accessed=4 * q.size * 2, transcendentals=q.size),
        name="attend",
    )(index, cont_len, q, do, ck, cv, pre)


def on_device(n_dp, n_t, cont_q, cont_k, cont_v, out_grad, prompt_k, prompt_v, cont_len, cont_prompt):
    slots = cont_q.shape[0]
    per, share = prompt_k.shape[:2]
    nz = n_dp // NY
    dp = lax.axis_index("dp")
    named = cont_prompt.reshape(n_dp, slots, 1)
    owner = lax.broadcasted_iota(jnp.int32, (1, 1, n_dp), 2)
    table = jnp.max(jnp.where(named // per == owner, named % per, -1), axis=1)
    mine = lax.dynamic_slice_in_dim(cont_prompt, dp * slots, slots) // per
    index = ((dp // NY - mine // NY + nz) % nz) * NY + (dp % NY - mine % NY + NY) % NY
    pre = gather_prompts(n_dp, n_t, table, prompt_k, prompt_v)
    out, dq, dk, dv, grads = attend(index, cont_len, cont_q, out_grad, cont_k, cont_v, pre)
    gk, gv = scatter_grads(n_dp, n_t, table, grads, per, share)
    return out, dq, dk, dv, gk, gv


def solution(mesh):
    n_dp, n_t = mesh.shape["dp"], mesh.shape["tensor"]
    return jax.shard_map(
        functools.partial(on_device, n_dp, n_t),
        mesh=mesh,
        in_specs=(
            P("dp", None, "tensor"),
            P("dp", None, "tensor"),
            P("dp", None, "tensor"),
            P("dp", None, "tensor"),
            P("dp", "tensor", None),
            P("dp", "tensor", None),
            P("dp"),
            P(),
        ),
        out_specs=(
            P("dp", None, "tensor"),
            P("dp", None, "tensor"),
            P("dp", None, "tensor"),
            P("dp", None, "tensor"),
            P("dp", "tensor", None),
            P("dp", "tensor", None),
        ),
        check_vma=False,
    )
```

time: 714 us -> 140 us (0.20)
  waiting for transfers between devices: 536 us -> 0 us
  Pallas kernels: 0 us -> 127 us
  local copies, waits for them, and re-layouts: 65.1 us -> 9.16 us
  matrix products: 45.1 us -> 0 us
  blocking collectives: 20.1 us -> 0 us
  starting transfers between devices: 20.1 us -> 0 us
  between operations: 14.1 us -> 0.73 us
  other arithmetic: 12.4 us -> 2.45 us
    reduce_scatter x2 -> x0, waiting for transfers between devices: 385 us -> none  [the longest x1 214 us: on_device(): lax.psum_scatter(table_v.astype(jnp.bfloat16), 'dp', scatter_dimension=0,...]
    all_gather x2 -> x0, waiting for transfers between devices: 146 us -> none  [the longest x1 81.5 us: on_device(): lax.all_gather(head_v, 'dp', axis=0, tiled=True)]
    pallas_call x0 -> x3, Pallas kernels: none -> 127 us  [the longest x1 60.6 us: scatter_grads(): pl.pallas_call(functools.partial(scatter_kernel, n_dp, n_t), out_shape=(o...]
    dot_general x8 -> x0, matrix products: 45.1 us -> none  [the longest x1 11.1 us: attend(): jnp.einsum('shglk,slhgd->skhd', weights, masked, preferred_element_type=j...]
    all_to_all x2 -> x0, blocking collectives: 20.1 us -> none  [the longest x1 11.2 us: on_device(): lax.all_to_all(prompt_k, 'tensor', split_axis=2, concat_axis=1, tiled=True)]
    all_to_all x2 -> x0, starting transfers between devices: 19.5 us -> none  [the longest x1 9.75 us: on_device(): lax.all_to_all(owned_k.astype(jnp.bfloat16), 'tensor', split_axis=1, conc...]
    convert_element_type x9 -> x0, local copies, waits for them, and re-layouts: 19 us -> none  [the longest x1 4.37 us: on_device(): table_v.astype(jnp.bfloat16)]
    unnamed x34 -> x16, local copies, waits for them, and re-layouts: 20.6 us -> 8.7 us
  transfers between devices with their start and end apart: 6 -> 0, of which waited for: 5 -> 0; matrix products, arithmetic and copies ran while one was open for 9% -> 0% of each run, Pallas kernels for 0% -> 0%
where the time goes in v1:
time: 140 us
  Pallas kernels  127 us (91%)
  local copies, waits for them, and re-layouts  9.16 us (7%)
  other arithmetic  2.45 us (2%)
    pallas_call x1, Pallas kernels, scatter_grads(): pl.pallas_call(functools.partial(scatter_kernel, n_dp, n_t), out_shape=(o...  60.6 us
    pallas_call x1, Pallas kernels, gather_prompts(): pl.pallas_call(functools.partial(gather_kernel, n_dp, n_t), out_shape=jax...  51.7 us
    pallas_call x1, Pallas kernels, attend(): pl.pallas_call(functools.partial(attend_kernel, batch), grid_spec=pltpu.P...  14.9 us
    unnamed x16, local copies, waits for them, and re-layouts  8.7 us

profile of v1, /device:TPU:1, one launch (start us, length us, event | category | flops | bytes accessed | tf_op | source)
XLA Modules:
  0.0 139.6 jit_solution(4444691177584177609)
XLA Ops:
  0.6 0.0 copy-start.6
  0.7 0.8 fusion.index_ref
  1.5 0.7 sign_compare_fusion
  2.1 0.1 ne.102
  2.3 0.7 broadcast_divide_fusion
  3.0 0.1 div.47
  3.1 0.1 rem.133
  3.2 0.1 copy.14
  3.3 0.1 copy.15
  3.3 0.2 select_reduce_fusion.m_ref
  3.6 0.0 copy-start
  3.6 0.9 copy-done
  4.5 0.0 copy-start.1
  4.5 0.9 copy-done.1
  5.4 51.7 %gather_prompts.1.pre_ref = bf16[32,2,128,128]{3,2,1,0:T(8,128)(2,1)S(1)} custom-call(s32[32,32]{1,0:T(8,128)S(1)} %select_reduce_fusion.m_ref, bf16[5,16,1024]{2,1,0:T(8,128)(2,1)S(1)} %copy-done, bf16[5,16,1024]{2,1,0:T(8,128)(2,1)S(1)} %copy-done.1), custom_call_target="tpu_custom_call" | custom-call | tf_op jit(solution)/shard_map/gather_prompts/pallas_call | solution.py:200
  57.2 0.0 copy-done.6
  57.2 0.0 copy-start.2
  57.2 1.7 %copy-done.2 = bf16[20,64,1024]{2,1,0:T(8,128)(2,1)S(1)} copy-done((bf16[20,64,1024]{2,1,0:T(8,128)(2,1)S(1)}, bf16[20,64,1024]{2,1,0:T(8,128)(2,1)}, u32[]{:S(2)}) %copy-start.2) | copy-done | bytes 2621464
  58.9 0.0 copy-start.3
  58.9 1.7 %copy-done.3 = bf16[20,64,1024]{2,1,0:T(8,128)(2,1)S(1)} copy-done((bf16[20,64,1024]{2,1,0:T(8,128)(2,1)S(1)}, bf16[20,64,1024]{2,1,0:T(8,128)(2,1)}, u32[]{:S(2)}) %copy-start.3) | copy-done | bytes 2621464
  60.7 0.0 copy-start.4
  60.7 1.0 copy-done.4
  61.7 0.0 copy-start.5
  61.7 1.0 copy-done.5
  62.6 14.9 %attend.1 = (bf16[20,64,1024]{2,1,0:T(8,128)(2,1)}, bf16[20,64,1024]{2,1,0:T(8,128)(2,1)}, bf16[20,64,128]{2,1,0:T(8,128)(2,1)}, bf16[20,64,128]{2,1,0:T(8,128)(2,1)}, bf16[32,2,128,128]{3,2,1,0:T(8,128)(2,1)S(1)}) custom-call(s32[20]{0:T(128)S(1)} %fusion.index_ref, s32[20]{0:T(128)S(1)} %copy-done.6, bf16[20,64,1024]{2,1,0:T(8,128)(2,1)S(1)} %copy-done.2, ...), custom_call_target="tpu_custom_call" | custom-call | flops 3019898880 | bytes 10485760 | tf_op jit(solution)/shard_map/attend/pallas_call | solution.py:467
  77.5 60.6 %scatter_grads.1 = (f32[5,16,1024]{2,1,0:T(8,128)S(1)}, f32[5,16,1024]{2,1,0:T(8,128)S(1)}) custom-call(s32[32,32]{1,0:T(8,128)S(1)} %select_reduce_fusion.m_ref, bf16[32,2,128,128]{3,2,1,0:T(8,128)(2,1)S(1)} %get-tuple-element.17.g_ref), custom_call_target="tpu_custom_call" | custom-call | tf_op jit(solution)/shard_map/scatter_grads/pallas_call | solution.py:372
  138.1 0.7 copy.18
  138.9 0.7 copy.19
  (1 shorter events, 0.0 us)
Async XLA Ops:
  0.6 56.6 %copy-start.6 = (s32[20]{0:T(128)S(1)}, s32[20]{0:T(128)}, u32[]{:S(2)}) copy-start(s32[20]{0:T(128)} %len_ref.1) | copy-start | bytes 244
  3.6 0.9 copy-start
  4.5 0.9 copy-start.1
  57.2 1.7 %copy-start.2 = (bf16[20,64,1024]{2,1,0:T(8,128)(2,1)S(1)}, bf16[20,64,1024]{2,1,0:T(8,128)(2,1)}, u32[]{:S(2)}) copy-start(bf16[20,64,1024]{2,1,0:T(8,128)(2,1)} %q_ref.1) | copy-start | bytes 7864324
  58.9 1.7 %copy-start.3 = (bf16[20,64,1024]{2,1,0:T(8,128)(2,1)S(1)}, bf16[20,64,1024]{2,1,0:T(8,128)(2,1)}, u32[]{:S(2)}) copy-start(bf16[20,64,1024]{2,1,0:T(8,128)(2,1)} %do_ref.1) | copy-start | bytes 7864324
  60.7 1.0 copy-start.4
  61.7 1.0 copy-start.5

commit v2 on v1

v2 whole, which is shorter than its diff:
```python
import functools
import math

import jax
import jax.numpy as jnp
from jax import lax
from jax.experimental import pallas as pl
from jax.experimental.pallas import tpu as pltpu
from jax.sharding import PartitionSpec as P

HD = 128
NY = 4
NEG = -1e30
VMEM_LIMIT = 56 * 2**20
MESH = pl.DeviceIdType.MESH
BF16 = jnp.bfloat16
F32 = jnp.float32


def coordinates(n_dp, n_t):
    dp = lax.axis_index("dp")
    t = lax.axis_index("tensor")
    z, y = dp // NY, dp % NY
    nz = n_dp // NY

    def at_z(step):
        return (lax.rem(z + step + nz, nz) * NY + y, t)

    def at_y(step):
        return (z * NY + lax.rem(y + step + NY, NY), t)

    def at_t(step):
        return (dp, lax.rem(t + step + n_t, n_t))

    def at_zy(step, u):
        return (lax.rem(z + step + nz, nz) * NY + lax.rem(y + u + NY, NY), t)

    return z, y, t, at_z, at_y, at_t, at_zy


def greet(devices):
    barrier = pltpu.get_barrier_semaphore()
    for device in devices:
        pl.semaphore_signal(barrier, inc=1, device_id=device, device_id_type=MESH)
    pl.semaphore_wait(barrier, len(devices))


def remote(src, dst, send, recv, device):
    return pltpu.make_async_remote_copy(
        src_ref=src,
        dst_ref=dst,
        send_sem=send,
        recv_sem=recv,
        device_id=device,
        device_id_type=MESH,
    )


def partners(n_t, at_z, at_y, at_t, at_zy):
    return (
        [at_t(j) for j in range(1, n_t)]
        + [at_y(u) for u in range(1, NY)]
        + [at_zy(way, u) for way in (1, -1) for u in range(NY)]
    )


def gather_kernel(n_dp, n_t, m_ref, pk_ref, pv_ref, out_ref, *scratch):
    nz = n_dp // NY
    half = nz // 2
    blocks = [list(scratch[:nz]), list(scratch[nz : 2 * nz])]
    picked, xs, xr, xl, zs, zr, ys, yr, yl = scratch[2 * nz :]
    z, y, t, at_z, at_y, at_t, at_zy = coordinates(n_dp, n_t)
    share = pk_ref.shape[1]
    greet(partners(n_t, at_z, at_y, at_t, at_zy))
    sent = []

    def start(*args):
        copy = remote(*args)
        copy.start()
        sent.append(copy)

    mine = pl.ds(pl.multiple_of(t * share, share), share)
    own = pl.ds(pl.multiple_of(t * HD, HD), HD)
    local = []
    for kv, ref in enumerate((pk_ref, pv_ref)):
        for j in range(1, n_t):
            to = at_t(j)
            cols = pl.ds(pl.multiple_of(to[1] * HD, HD), HD)
            start(ref.at[:, :, cols], blocks[kv][0].at[:, mine, :], xs.at[kv, j], xr.at[kv, j], to)
        local.append(pltpu.make_async_copy(ref.at[:, :, own], blocks[kv][0].at[:, mine, :], xl.at[kv]))
        local[kv].start()

    def wait_own(kv):
        local[kv].wait()
        for j in range(1, n_t):
            rows = pl.ds(pl.multiple_of(at_t(-j)[1] * share, share), share)
            remote(
                (pk_ref, pv_ref)[kv].at[:, :, own], blocks[kv][0].at[:, rows, :], xs.at[kv, j], xr.at[kv, j], at_t(j)
            ).wait_recv()

    def push(kv, r, way):
        nxt = (r + way) % nz
        start(blocks[kv][r], blocks[kv][nxt], zs.at[kv, nxt], zr.at[kv, nxt], at_z(way))

    def wait_block(kv, r):
        remote(blocks[kv][r], blocks[kv][r], zs.at[kv, r], zr.at[kv, r], at_z(1)).wait_recv()

    def spread(kv, r, way):
        row = lax.rem(z - r + nz, nz)
        there = (r + way) % nz
        for u in (2, 1, 3, 0):
            to = at_zy(way, u)
            pick = jnp.maximum(m_ref[to[0], row * NY + y], 0)
            picked[there, u, kv] = blocks[kv][r][pick]
            place = out_ref.at[there * NY + u, kv]
            if u == 0 and way == 0:
                copy = pltpu.make_async_copy(picked.at[there, u, kv], place, yl.at[there, kv])
                copy.start()
                local.append(copy)
            else:
                start(picked.at[there, u, kv], place, ys.at[there, u, kv], yr.at[there, u, kv], to)

    for kv in range(2):
        wait_own(kv)
        push(kv, 0, 1)
        push(kv, 0, -1)
    for kv in range(2):
        spread(kv, 0, 0)
    for h in range(1, half):
        for kv in range(2):
            for r, way in ((h, 1), (nz - h, -1)):
                wait_block(kv, r)
                if h < half - 1:
                    push(kv, r, way)
                elif kv == (0 if way == 1 else 1):
                    spread(kv, r, way)
        for kv in range(2):
            for r in (h, nz - h):
                spread(kv, r, 0)
    for copy in local[2:]:
        copy.wait()
    for copy in sent:
        copy.wait_send()
    for r in range(nz):
        for u in range(NY):
            for kv in range(2):
                if u or r == half:
                    place = out_ref.at[r * NY + u, kv]
                    remote(
                        picked.at[r, u, kv], place, ys.at[r, u, kv], yr.at[r, u, kv], at_y(1)
                    ).wait_recv()


def gather_prompts(n_dp, n_t, table, pk, pv, cid=0):
    nz = n_dp // NY
    per, share, width = pk.shape
    plen = share * n_t
    dma = pltpu.SemaphoreType.DMA
    return pl.pallas_call(
        functools.partial(gather_kernel, n_dp, n_t),
        out_shape=jax.ShapeDtypeStruct((n_dp, 2, plen, HD), BF16),
        in_specs=[
            pl.BlockSpec(memory_space=pltpu.SMEM),
            pl.BlockSpec(memory_space=pl.ANY),
            pl.BlockSpec(memory_space=pl.ANY),
        ],
        out_specs=pl.BlockSpec(memory_space=pl.ANY),
        scratch_shapes=[pltpu.VMEM((per, plen, HD), BF16) for _ in range(2 * nz)]
        + [
            pltpu.VMEM((nz, NY, 2, plen, HD), BF16),
            dma((2, n_t)),
            dma((2, n_t)),
            dma((2,)),
            dma((2, nz)),
            dma((2, nz)),
            dma((nz, NY, 2)),
            dma((nz, NY, 2)),
            dma((nz, 2)),
        ],
        compiler_params=pltpu.CompilerParams(
            collective_id=cid, has_side_effects=True, vmem_limit_bytes=VMEM_LIMIT
        ),
        name="gather_prompts",
    )(table, pk, pv)


def scatter_kernel(n_dp, n_t, m_ref, g_ref, ok_ref, ov_ref, *scratch):
    nz = n_dp // NY
    half = nz // 2
    arrived, far, chain, total, pieces, ys, yr, yl, fs, fr, zs, zr, xs, xr = scratch
    z, y, t, at_z, at_y, at_t, at_zy = coordinates(n_dp, n_t)
    per, share = ok_ref.shape[:2]
    greet(partners(n_t, at_z, at_y, at_t, at_zy))
    sent = []

    def start(*args):
        copy = remote(*args)
        copy.start()
        sent.append(copy)

    def send_far(kv):
        for u in range(NY):
            src = g_ref.at[half * NY + u, kv]
            start(src, far.at[kv, u], fs.at[kv, u], fr.at[kv, u], at_zy(-1 if kv == 0 else 1, -u))

    def wait_far(kv):
        for u in range(NY):
            src = g_ref.at[half * NY + u, kv]
            remote(src, far.at[kv, u], fs.at[kv, u], fr.at[kv, u], at_y(1)).wait_recv()

    def send_out(kv, r):
        for u in (2, 1, 3):
            start(g_ref.at[r * NY + u, kv], arrived.at[r, u, kv], ys.at[r, u, kv], yr.at[r, u, kv], at_y(-u))
        pltpu.make_async_copy(g_ref.at[r * NY, kv], arrived.at[r, 0, kv], yl.at[r, kv]).start()

    def wait_y(kv, r):
        pltpu.make_async_copy(g_ref.at[r * NY, kv], arrived.at[r, 0, kv], yl.at[r, kv]).wait()
        for u in range(1, NY):
            remote(
                g_ref.at[r * NY + u, kv], arrived.at[r, u, kv], ys.at[r, u, kv], yr.at[r, u, kv], at_y(1)
            ).wait_recv()

    def sums(kv, r, store, *more):
        row = lax.rem(z - r + nz, nz)
        column = row * NY + y
        parts = [(m_ref[at_y(u)[0], column], arrived.at[r, u, kv]) for u in range(NY)]
        if r == (half - 1 if kv == 0 else half + 1):
            way = 1 if kv == 0 else -1
            parts += [(m_ref[at_zy(way, u)[0], column], far.at[kv, u]) for u in range(NY)]
        for p in range(per):
            acc = None
            for which, ref in parts:
                piece = jnp.where(which == p, ref[...].astype(F32), 0.0)
                acc = piece if acc is None else acc + piece
            for ref in more:
                acc = acc + ref[p].astype(F32)
            store[p] = acc.astype(BF16)

    def wait_chain(d, kv, r):
        remote(
            chain.at[d, kv, r], chain.at[d, kv, r], zs.at[d, kv, r], zr.at[d, kv, r], at_z(1)
        ).wait_recv()

    def reduce_block(kv, r):
        d = 0 if r > half else 1
        buf = chain.at[d, kv, r]
        if r in (half - 1, half + 1):
            sums(kv, r, buf)
        else:
            wait_chain(d, kv, r)
            sums(kv, r, buf, buf)
        step = 1 if d == 0 else -1
        nxt = (r + step) % nz
        start(buf, chain.at[d, kv, nxt], zs.at[d, kv, nxt], zr.at[d, kv, nxt], at_z(step))

    for kv in range(2):
        send_far(kv)
        for r in (half - 1, half + 1):
            send_out(kv, r)
    for h in range(half - 1, 0, -1):
        for kv in range(2):
            for r in (h, nz - h):
                wait_y(kv, r)
            for r in (h - 1, nz - h + 1) if h > 1 else (0,):
                send_out(kv, r)
            if h == half - 1:
                wait_far(kv)
            for r in (h, nz - h):
                reduce_block(kv, r)
    mine = pl.ds(pl.multiple_of(t * share, share), share)
    own = pl.ds(pl.multiple_of(t * HD, HD), HD)
    for kv in range(2):
        wait_y(kv, 0)
        for d in range(2):
            wait_chain(d, kv, 0)
        sums(kv, 0, total.at[kv], chain.at[0, kv, 0], chain.at[1, kv, 0])
        for j in range(1, n_t):
            to = at_t(j)
            rows = pl.ds(pl.multiple_of(to[1] * share, share), share)
            start(total.at[kv, :, rows, :], pieces.at[kv, j], xs.at[kv, j], xr.at[kv, j], to)
        (ok_ref, ov_ref)[kv][:, :, own] = total[kv, :, mine, :].astype(F32)
    for kv in range(2):
        for j in range(1, n_t):
            remote(
                total.at[kv, :, mine, :], pieces.at[kv, j], xs.at[kv, j], xr.at[kv, j], at_t(j)
            ).wait_recv()
            cols = pl.ds(pl.multiple_of(at_t(-j)[1] * HD, HD), HD)
            (ok_ref, ov_ref)[kv][:, :, cols] = pieces[kv, j].astype(F32)
    for copy in sent:
        copy.wait_send()


def scatter_grads(n_dp, n_t, table, grads, per, share, cid=1):
    nz = n_dp // NY
    plen = share * n_t
    dma = pltpu.SemaphoreType.DMA
    out = jax.ShapeDtypeStruct((per, share, n_t * HD), F32)
    return pl.pallas_call(
        functools.partial(scatter_kernel, n_dp, n_t),
        out_shape=(out, out),
        in_specs=[
            pl.BlockSpec(memory_space=pltpu.SMEM),
            pl.BlockSpec(memory_space=pl.ANY),
        ],
        out_specs=[pl.BlockSpec(memory_space=pltpu.VMEM)] * 2,
        scratch_shapes=[
            pltpu.VMEM((nz, NY, 2, plen, HD), BF16),
            pltpu.VMEM((2, NY, plen, HD), BF16),
            pltpu.VMEM((2, 2, nz, per, plen, HD), BF16),
            pltpu.VMEM((2, per, plen, HD), BF16),
            pltpu.VMEM((2, n_t, per, share, HD), BF16),
            dma((nz, NY, 2)),
            dma((nz, NY, 2)),
            dma((nz, 2)),
            dma((2, NY)),
            dma((2, NY)),
            dma((2, 2, nz)),
            dma((2, 2, nz)),
            dma((2, n_t)),
            dma((2, n_t)),
        ],
        compiler_params=pltpu.CompilerParams(
            collective_id=cid, has_side_effects=True, vmem_limit_bytes=VMEM_LIMIT
        ),
        name="scatter_grads",
    )(table, grads)


def dot(a, b, dims):
    return lax.dot_general(a, b, (dims, ((), ())), preferred_element_type=F32)


def attend_slot(length, queries, cotangent, keys, values, heads):
    rows = queries.shape[0]
    count = keys.shape[0]
    tokens = rows // heads
    prefix = count - tokens
    scale = 1.0 / math.sqrt(HD)
    token = lax.rem(lax.broadcasted_iota(jnp.int32, (1, rows), 1), tokens)
    valid = lax.rem(lax.broadcasted_iota(jnp.int32, (rows, 1), 0), tokens) < length
    cotangent = jnp.where(valid, cotangent, jnp.zeros_like(cotangent))
    scores = dot(keys, queries, ((1,), (1,)))
    dweights = dot(values, cotangent, ((1,), (1,)))
    key = lax.broadcasted_iota(jnp.int32, (tokens, rows), 0)
    tail = jnp.where(key <= token, scores[prefix:], NEG)
    scores = jnp.concatenate([scores[:prefix], tail], axis=0)
    top = jnp.max(scores, axis=0, keepdims=True)
    exponent = jnp.exp2((scores - top) * (scale * math.log2(math.e)))
    probs = exponent * (1.0 / jnp.sum(exponent, axis=0, keepdims=True))
    weights = probs.astype(BF16)
    delta = jnp.sum(probs * dweights, axis=0, keepdims=True)
    dscores = (probs * (dweights - delta) * scale).astype(BF16)
    out = dot(weights, values, ((0,), (0,)))
    out = jnp.where(valid, out, 0.0).astype(BF16)
    dq = dot(dscores, keys, ((0,), (0,))).astype(BF16)
    dk = dot(dscores, queries, ((1,), (0,)))
    dv = dot(weights, cotangent, ((1,), (0,)))
    return out, dq, dk, dv


def attend_kernel(
    batch, per, named_ref, len_ref, q_ref, do_ref, ck_ref, cv_ref, pre_ref, out_ref, dq_ref, dk_ref, dv_ref, g_ref
):
    step = pl.program_id(0)
    dp = lax.axis_index("dp")
    slots = len_ref.shape[0]
    nz = pre_ref.shape[0] // NY
    heads = q_ref.shape[2] // HD
    tokens = q_ref.shape[1]
    prefix = pre_ref.shape[2]
    for b in range(batch):
        s = step * batch + b
        owner = named_ref[dp * slots + s] // per
        row = lax.rem(dp // NY - owner // NY + nz, nz)
        place = row * NY + lax.rem(dp % NY - owner % NY + NY, NY)
        queries = jnp.concatenate([q_ref[b, :, h * HD : (h + 1) * HD] for h in range(heads)], axis=0)
        cotangent = jnp.concatenate([do_ref[b, :, h * HD : (h + 1) * HD] for h in range(heads)], axis=0)
        keys = jnp.concatenate([pre_ref[place, 0], ck_ref[b]], axis=0)
        values = jnp.concatenate([pre_ref[place, 1], cv_ref[b]], axis=0)
        out, dq, dk, dv = attend_slot(len_ref[s], queries, cotangent, keys, values, heads)
        for h in range(heads):
            out_ref[b, :, h * HD : (h + 1) * HD] = out[h * tokens : (h + 1) * tokens]
            dq_ref[b, :, h * HD : (h + 1) * HD] = dq[h * tokens : (h + 1) * tokens]
        dk_ref[b] = dk[prefix:].astype(BF16)
        dv_ref[b] = dv[prefix:].astype(BF16)
        g_ref[place, 0] = dk[:prefix].astype(BF16)
        g_ref[place, 1] = dv[:prefix].astype(BF16)


def attend(per, named, cont_len, q, do, ck, cv, pre, batch=2):
    slots, tokens, width = q.shape
    wide = pl.BlockSpec((batch, tokens, width), lambda i, *_: (i, 0, 0))
    thin = pl.BlockSpec((batch, tokens, HD), lambda i, *_: (i, 0, 0))
    whole = pl.BlockSpec(pre.shape, lambda i, *_: (0, 0, 0, 0))
    flops = 12 * slots * tokens * (tokens + pre.shape[2]) * width
    return pl.pallas_call(
        functools.partial(attend_kernel, batch, per),
        grid_spec=pltpu.PrefetchScalarGridSpec(
            num_scalar_prefetch=2,
            grid=(slots // batch,),
            in_specs=[wide, wide, thin, thin, whole],
            out_specs=[wide, wide, thin, thin, whole],
        ),
        out_shape=(
            jax.ShapeDtypeStruct(q.shape, BF16),
            jax.ShapeDtypeStruct(q.shape, BF16),
            jax.ShapeDtypeStruct(ck.shape, BF16),
            jax.ShapeDtypeStruct(cv.shape, BF16),
            jax.ShapeDtypeStruct(pre.shape, BF16),
        ),
        compiler_params=pltpu.CompilerParams(vmem_limit_bytes=VMEM_LIMIT),
        cost_estimate=pl.CostEstimate(flops=flops, bytes_accessed=4 * q.size * 2, transcendentals=q.size),
        name="attend",
    )(named, cont_len, q, do, ck, cv, pre)


def on_device(n_dp, n_t, cont_q, cont_k, cont_v, out_grad, prompt_k, prompt_v, cont_len, cont_prompt):
    slots = cont_q.shape[0]
    per, share = prompt_k.shape[:2]
    owner = lax.broadcasted_iota(jnp.int32, (1, 1, n_dp), 2)
    offset = cont_prompt.reshape(n_dp, slots, 1) - owner * per
    table = jnp.max(jnp.where((offset >= 0) & (offset < per), offset, -1), axis=1)
    pre = gather_prompts(n_dp, n_t, table, prompt_k, prompt_v)
    out, dq, dk, dv, grads = attend(per, cont_prompt, cont_len, cont_q, out_grad, cont_k, cont_v, pre)
    gk, gv = scatter_grads(n_dp, n_t, table, grads, per, share)
    return out, dq, dk, dv, gk, gv


def solution(mesh):
    n_dp, n_t = mesh.shape["dp"], mesh.shape["tensor"]
    return jax.shard_map(
        functools.partial(on_device, n_dp, n_t),
        mesh=mesh,
        in_specs=(
            P("dp", None, "tensor"),
            P("dp", None, "tensor"),
            P("dp", None, "tensor"),
            P("dp", None, "tensor"),
            P("dp", "tensor", None),
            P("dp", "tensor", None),
            P("dp"),
            P(),
        ),
        out_specs=(
            P("dp", None, "tensor"),
            P("dp", None, "tensor"),
            P("dp", None, "tensor"),
            P("dp", None, "tensor"),
            P("dp", "tensor", None),
            P("dp", "tensor", None),
        ),
        check_vma=False,
    )
```

time: 140 us -> 118 us (0.84)
  Pallas kernels: 127 us -> 112 us
  local copies, waits for them, and re-layouts: 9.16 us -> 4.3 us
  other arithmetic: 2.45 us -> 0.78 us
    pallas_call x1, Pallas kernels: 60.6 us -> 43.4 us  [scatter_grads(): pl.pallas_call(functools.partial(scatter_kernel, n_dp, n_t), out_shape=(o...]
    unnamed x16 -> x2, local copies, waits for them, and re-layouts: 8.7 us -> 3.44 us
    pallas_call x1, Pallas kernels: 14.9 us -> 17.9 us  [attend(): pl.pallas_call(functools.partial(attend_kernel, batch, per), grid_spec=pl...]
where the time goes in v2:
time: 118 us
  Pallas kernels  112 us (95%)
  local copies, waits for them, and re-layouts  4.3 us (4%)
    pallas_call x1, Pallas kernels, gather_prompts(): pl.pallas_call(functools.partial(gather_kernel, n_dp, n_t), out_shape=jax...  50.9 us
    pallas_call x1, Pallas kernels, scatter_grads(): pl.pallas_call(functools.partial(scatter_kernel, n_dp, n_t), out_shape=(o...  43.4 us
    pallas_call x1, Pallas kernels, attend(): pl.pallas_call(functools.partial(attend_kernel, batch, per), grid_spec=pl...  17.9 us
    unnamed x2, local copies, waits for them, and re-layouts  3.44 us

profile of v2, /device:TPU:1, one launch (start us, length us, event | category | flops | bytes accessed | tf_op | source)
XLA Modules:
  0.0 118.0 jit_solution(1024620712259571936)
XLA Ops:
  0.6 0.8 sub.15
  1.4 0.1 copy.14
  1.5 0.8 fusion.m_ref
  2.3 50.9 %gather_prompts.1.pre_ref = bf16[32,2,128,128]{3,2,1,0:T(8,128)(2,1)} custom-call(s32[32,32]{1,0:T(8,128)} %fusion.m_ref, bf16[5,16,1024]{2,1,0:T(8,128)(2,1)} %pk_ref.1, bf16[5,16,1024]{2,1,0:T(8,128)(2,1)} %pv_ref.1), custom_call_target="tpu_custom_call" | custom-call | tf_op jit(solution)/shard_map/gather_prompts/pallas_call | solution.py:159
  53.2 17.9 %attend.1 = (bf16[20,64,1024]{2,1,0:T(8,128)(2,1)}, bf16[20,64,1024]{2,1,0:T(8,128)(2,1)}, bf16[20,64,128]{2,1,0:T(8,128)(2,1)}, bf16[20,64,128]{2,1,0:T(8,128)(2,1)}, bf16[32,2,128,128]{3,2,1,0:T(8,128)(2,1)}) custom-call(s32[640]{0:T(1024)} %named_ref.1, s32[20]{0:T(128)} %len_ref.1, bf16[20,64,1024]{2,1,0:T(8,128)(2,1)} %q_ref.1, ...), custom_call_target="tpu_custom_call" | custom-call | flops 3019898880 | bytes 10485760 | tf_op jit(solution)/shard_map/attend/pallas_call | solution.py:396
  71.1 43.4 %scatter_grads.1 = (f32[5,16,1024]{2,1,0:T(8,128)}, f32[5,16,1024]{2,1,0:T(8,128)}) custom-call(s32[32,32]{1,0:T(8,128)} %fusion.m_ref, bf16[32,2,128,128]{3,2,1,0:T(8,128)(2,1)} %get-tuple-element.17.g_ref), custom_call_target="tpu_custom_call" | custom-call | tf_op jit(solution)/shard_map/scatter_grads/pallas_call | solution.py:298
  114.5 1.7 %copy.17 = f32[5,16,1024]{2,1,0:T(8,128)} copy(f32[5,16,1024]{2,1,0:T(8,128)} %get-tuple-element.30) | data formatting | bytes 655360
  116.2 1.7 %copy.18 = f32[5,16,1024]{2,1,0:T(8,128)} copy(f32[5,16,1024]{2,1,0:T(8,128)} %get-tuple-element.31) | data formatting | bytes 655360
  (1 shorter events, 0.0 us)

commit v3 on v2

--- a/solution.py
+++ b/solution.py
@@ -10,8 +10,10 @@
 
 HD = 128
 NY = 4
+PACK = 8
 NEG = -1e30
 VMEM_LIMIT = 56 * 2**20
+FINISH_LIMIT = 56 * 2**20
 MESH = pl.DeviceIdType.MESH
 BF16 = jnp.bfloat16
 F32 = jnp.float32
@@ -83,6 +85,9 @@
     own = pl.ds(pl.multiple_of(t * HD, HD), HD)
     local = []
     for kv, ref in enumerate((pk_ref, pv_ref)):
+        for copy in sent:
+            copy.wait_send()
+        sent.clear()
         for j in range(1, n_t):
             to = at_t(j)
             cols = pl.ds(pl.multiple_of(to[1] * HD, HD), HD)
@@ -110,7 +115,7 @@
         there = (r + way) % nz
         for u in (2, 1, 3, 0):
             to = at_zy(way, u)
-            pick = jnp.maximum(m_ref[to[0], row * NY + y], 0)
+            pick = lax.rem(jnp.maximum(m_ref[to[0], row * NY + y], 0), PACK)
             picked[there, u, kv] = blocks[kv][r][pick]
             place = out_ref.at[there * NY + u, kv]
             if u == 0 and way == 0:
@@ -134,7 +139,6 @@
                     push(kv, r, way)
                 elif kv == (0 if way == 1 else 1):
                     spread(kv, r, way)
-        for kv in range(2):
             for r in (h, nz - h):
                 spread(kv, r, 0)
     for copy in local[2:]:
@@ -184,57 +188,89 @@
     )(table, pk, pv)
 
 
-def scatter_kernel(n_dp, n_t, m_ref, g_ref, ok_ref, ov_ref, *scratch):
+def attend_scatter_kernel(
+    n_dp, n_t, m_ref, len_ref, q_ref, do_ref, ck_ref, cv_ref, pre_ref, out_ref, dq_ref, tail_ref, ok_ref, ov_ref, *scratch
+):
     nz = n_dp // NY
     half = nz // 2
-    arrived, far, chain, total, pieces, ys, yr, yl, fs, fr, zs, zr, xs, xr = scratch
+    qb, dob, ckb, cvb, preb, ob, dqb, tailb, g_ref = scratch[:9]
+    arrived, far, chain, term, total, pieces, ins, pres, outs, ys, yr, yl, fs, fr, zs, zr, xs, xr = scratch[9:]
     z, y, t, at_z, at_y, at_t, at_zy = coordinates(n_dp, n_t)
     per, share = ok_ref.shape[:2]
+    dp = z * NY + y
+    slots, tokens, width = q_ref.shape
+    heads = width // HD
+    prefix = pre_ref.shape[2]
+    local = [
+        pltpu.make_async_copy(src, dst, ins.at[i])
+        for i, (src, dst) in enumerate(((q_ref, qb), (do_ref, dob), (ck_ref, ckb), (cv_ref, cvb)))
+    ]
+
+    def prompts(r):
+        return pltpu.make_async_copy(pre_ref.at[pl.ds(r * NY, NY)], preb.at[pl.ds(r * NY, NY)], pres.at[r])
+
+    def results(r):
+        part = pl.ds(r * NY, NY)
+        return [
+            pltpu.make_async_copy(src.at[part], dst.at[part], outs.at[i, r])
+            for i, (src, dst) in enumerate(((ob, out_ref), (dqb, dq_ref), (tailb, tail_ref)))
+        ]
+
+    for copy in local:
+        copy.start()
+    order = [half]
+    for h in range(half - 1, 0, -1):
+        order += [h, nz - h]
+    order.append(0)
+    for r in order:
+        prompts(r).start()
     greet(partners(n_t, at_z, at_y, at_t, at_zy))
-    sent = []
-
-    def start(*args):
-        copy = remote(*args)
-        copy.start()
-        sent.append(copy)
-
-    def send_far(kv):
-        for u in range(NY):
-            src = g_ref.at[half * NY + u, kv]
-            start(src, far.at[kv, u], fs.at[kv, u], fr.at[kv, u], at_zy(-1 if kv == 0 else 1, -u))
-
-    def wait_far(kv):
-        for u in range(NY):
-            src = g_ref.at[half * NY + u, kv]
-            remote(src, far.at[kv, u], fs.at[kv, u], fr.at[kv, u], at_y(1)).wait_recv()
+
+    def far_copy(kv, u):
+        src = g_ref.at[half * NY + u, kv]
+        return remote(src, far.at[kv, u], fs.at[kv, u], fr.at[kv, u], at_zy(-1 if kv == 0 else 1, -u))
+
+    def out_copy(kv, r, u):
+        return remote(
+            g_ref.at[r * NY + u, kv], arrived.at[r, u, kv], ys.at[r, u, kv], yr.at[r, u, kv], at_y(-u)
+        )
+
+    def chain_copy(kv, r):
+        d = 0 if r > half else 1
+        step = 1 if d == 0 else -1
+        nxt = (r + step) % nz
+        return remote(
+            chain.at[d, kv, r], chain.at[d, kv, nxt], zs.at[d, kv, nxt], zr.at[d, kv, nxt], at_z(step)
+        )
+
+    def piece_copy(kv, j):
+        to = at_t(j)
+        rows = pl.ds(pl.multiple_of(to[1] * share, share), share)
+        return remote(total.at[kv, :, rows, :], pieces.at[kv, j], xs.at[kv, j], xr.at[kv, j], to)
 
     def send_out(kv, r):
         for u in (2, 1, 3):
-            start(g_ref.at[r * NY + u, kv], arrived.at[r, u, kv], ys.at[r, u, kv], yr.at[r, u, kv], at_y(-u))
+            out_copy(kv, r, u).start()
         pltpu.make_async_copy(g_ref.at[r * NY, kv], arrived.at[r, 0, kv], yl.at[r, kv]).start()
 
     def wait_y(kv, r):
         pltpu.make_async_copy(g_ref.at[r * NY, kv], arrived.at[r, 0, kv], yl.at[r, kv]).wait()
         for u in range(1, NY):
-            remote(
-                g_ref.at[r * NY + u, kv], arrived.at[r, u, kv], ys.at[r, u, kv], yr.at[r, u, kv], at_y(1)
-            ).wait_recv()
-
-    def sums(kv, r, store, *more):
+            out_copy(kv, r, u).wait_recv()
+
+    def sums(kv, r, store):
         row = lax.rem(z - r + nz, nz)
         column = row * NY + y
-        parts = [(m_ref[at_y(u)[0], column], arrived.at[r, u, kv]) for u in range(NY)]
+        parts = [(lax.rem(m_ref[at_y(u)[0], column], PACK), arrived.at[r, u, kv]) for u in range(NY)]
         if r == (half - 1 if kv == 0 else half + 1):
             way = 1 if kv == 0 else -1
-            parts += [(m_ref[at_zy(way, u)[0], column], far.at[kv, u]) for u in range(NY)]
+            parts += [(lax.rem(m_ref[at_zy(way, u)[0], column], PACK), far.at[kv, u]) for u in range(NY)]
         for p in range(per):
             acc = None
             for which, ref in parts:
                 piece = jnp.where(which == p, ref[...].astype(F32), 0.0)
                 acc = piece if acc is None else acc + piece
-            for ref in more:
-                acc = acc + ref[p].astype(F32)
-            store[p] = acc.astype(BF16)
+            store[p] = acc.astype(store.dtype)
 
     def wait_chain(d, kv, r):
         remote(
@@ -247,68 +283,132 @@
         if r in (half - 1, half + 1):
             sums(kv, r, buf)
         else:
+            sums(kv, r, term.at[d])
             wait_chain(d, kv, r)
-            sums(kv, r, buf, buf)
-        step = 1 if d == 0 else -1
-        nxt = (r + step) % nz
-        start(buf, chain.at[d, kv, nxt], zs.at[d, kv, nxt], zr.at[d, kv, nxt], at_z(step))
-
-    for kv in range(2):
-        send_far(kv)
-        for r in (half - 1, half + 1):
-            send_out(kv, r)
-    for h in range(half - 1, 0, -1):
+            buf[...] = (buf[...].astype(F32) + term[d]).astype(BF16)
+        chain_copy(kv, r).start()
+
+    def compute(r):
+        row = lax.rem(z - r + nz, nz)
+        prompts(r).wait()
+        for u in range(NY):
+            w = r * NY + u
+            slot = lax.div(jnp.maximum(m_ref[dp, row * NY + lax.rem(y - u + NY, NY)], 0), PACK)
+            queries = jnp.concatenate([qb[slot, :, h * HD : (h + 1) * HD] for h in range(heads)], axis=0)
+            cotangent = jnp.concatenate([dob[slot, :, h * HD : (h + 1) * HD] for h in range(heads)], axis=0)
+            keys = jnp.concatenate([preb[w, 0], ckb[slot]], axis=0)
+            values = jnp.concatenate([preb[w, 1], cvb[slot]], axis=0)
+            out, dq, dk, dv = attend_slot(len_ref[slot], queries, cotangent, keys, values, heads)
+            for h in range(heads):
+                ob[w, :, h * HD : (h + 1) * HD] = out[h * tokens : (h + 1) * tokens]
+                dqb[w, :, h * HD : (h + 1) * HD] = dq[h * tokens : (h + 1) * tokens]
+            g_ref[w, 0] = dk[:prefix]
+            g_ref[w, 1] = dv[:prefix]
+            tailb[w, 0] = dk[prefix:]
+            tailb[w, 1] = dv[prefix:]
+        for copy in results(r):
+            copy.start()
+
+    def hop(h):
         for kv in range(2):
             for r in (h, nz - h):
                 wait_y(kv, r)
-            for r in (h - 1, nz - h + 1) if h > 1 else (0,):
-                send_out(kv, r)
             if h == half - 1:
-                wait_far(kv)
+                for u in range(NY):
+                    far_copy(kv, u).wait_recv()
             for r in (h, nz - h):
                 reduce_block(kv, r)
+
+    def after(i):
+        if i == 0:
+            for kv in range(2):
+                for u in range(NY):
+                    far_copy(kv, u).start()
+            return
+        for kv in range(2):
+            send_out(kv, order[i])
+        if i >= 4 and i % 2 == 0:
+            hop(half + 1 - i // 2)
+
+    def step(i, carry):
+        back = lax.div(i + 1, 2)
+        sign = 2 * lax.rem(i + 1, 2) - 1
+        compute(lax.rem(half + sign * back + nz, nz))
+        for j in range(nz):
+            pl.when(i == j)(functools.partial(after, j))
+        return carry
+
+    for copy in local:
+        copy.wait()
+    lax.fori_loop(0, nz, step, 0)
+    hop(1)
     mine = pl.ds(pl.multiple_of(t * share, share), share)
     own = pl.ds(pl.multiple_of(t * HD, HD), HD)
     for kv in range(2):
         wait_y(kv, 0)
+        sums(kv, 0, term.at[0])
         for d in range(2):
             wait_chain(d, kv, 0)
-        sums(kv, 0, total.at[kv], chain.at[0, kv, 0], chain.at[1, kv, 0])
+        total[kv] = (term[0] + chain[0, kv, 0].astype(F32) + chain[1, kv, 0].astype(F32)).astype(BF16)
         for j in range(1, n_t):
-            to = at_t(j)
-            rows = pl.ds(pl.multiple_of(to[1] * share, share), share)
-            start(total.at[kv, :, rows, :], pieces.at[kv, j], xs.at[kv, j], xr.at[kv, j], to)
+            piece_copy(kv, j).start()
         (ok_ref, ov_ref)[kv][:, :, own] = total[kv, :, mine, :].astype(F32)
     for kv in range(2):
         for j in range(1, n_t):
-            remote(
-                total.at[kv, :, mine, :], pieces.at[kv, j], xs.at[kv, j], xr.at[kv, j], at_t(j)
-            ).wait_recv()
+            piece_copy(kv, j).wait_recv()
             cols = pl.ds(pl.multiple_of(at_t(-j)[1] * HD, HD), HD)
             (ok_ref, ov_ref)[kv][:, :, cols] = pieces[kv, j].astype(F32)
-    for copy in sent:
-        copy.wait_send()
-
-
-def scatter_grads(n_dp, n_t, table, grads, per, share, cid=1):
+    for kv in range(2):
+        for u in range(NY):
+            far_copy(kv, u).wait_send()
+        for r in order[1:]:
+            for u in range(1, NY):
+                out_copy(kv, r, u).wait_send()
+            if r:
+                chain_copy(kv, r).wait_send()
+        for j in range(1, n_t):
+            piece_copy(kv, j).wait_send()
+    for r in range(nz):
+        for copy in results(r):
+            copy.wait()
+
+
+def attend_scatter(n_dp, n_t, table, cont_len, q, do, ck, cv, pre, per, share, cid=1):
     nz = n_dp // NY
-    plen = share * n_t
+    slots, tokens, width = q.shape
+    plen = pre.shape[2]
     dma = pltpu.SemaphoreType.DMA
-    out = jax.ShapeDtypeStruct((per, share, n_t * HD), F32)
+    shape = jax.ShapeDtypeStruct
+    anywhere = pl.BlockSpec(memory_space=pl.ANY)
+    scalars = pl.BlockSpec(memory_space=pltpu.SMEM)
+    part = shape((per, share, n_t * HD), F32)
+    wide = (n_dp, tokens, width)
+    tails = (n_dp, 2, tokens, HD)
+    flops = 12 * n_dp * tokens * (tokens + plen) * width
     return pl.pallas_call(
-        functools.partial(scatter_kernel, n_dp, n_t),
-        out_shape=(out, out),
-        in_specs=[
-            pl.BlockSpec(memory_space=pltpu.SMEM),
-            pl.BlockSpec(memory_space=pl.ANY),
-        ],
-        out_specs=[pl.BlockSpec(memory_space=pltpu.VMEM)] * 2,
+        functools.partial(attend_scatter_kernel, n_dp, n_t),
+        out_shape=(shape(wide, BF16), shape(wide, BF16), shape(tails, BF16), part, part),
+        in_specs=[scalars, scalars] + [anywhere] * 5,
+        out_specs=[anywhere] * 3 + [pl.BlockSpec(memory_space=pltpu.VMEM)] * 2,
         scratch_shapes=[
+            pltpu.VMEM(q.shape, BF16),
+            pltpu.VMEM(q.shape, BF16),
+            pltpu.VMEM(ck.shape, BF16),
+            pltpu.VMEM(ck.shape, BF16),
+            pltpu.VMEM(pre.shape, BF16),
+            pltpu.VMEM(wide, BF16),
+            pltpu.VMEM(wide, BF16),
+            pltpu.VMEM(tails, BF16),
+            pltpu.VMEM(pre.shape, BF16),
             pltpu.VMEM((nz, NY, 2, plen, HD), BF16),
             pltpu.VMEM((2, NY, plen, HD), BF16),
             pltpu.VMEM((2, 2, nz, per, plen, HD), BF16),
+            pltpu.VMEM((2, per, plen, HD), F32),
             pltpu.VMEM((2, per, plen, HD), BF16),
             pltpu.VMEM((2, n_t, per, share, HD), BF16),
+            dma((4,)),
+            dma((nz,)),
+            dma((3, nz)),
             dma((nz, NY, 2)),
             dma((nz, NY, 2)),
             dma((nz, 2)),
@@ -322,8 +422,84 @@
         compiler_params=pltpu.CompilerParams(
             collective_id=cid, has_side_effects=True, vmem_limit_bytes=VMEM_LIMIT
         ),
-        name="scatter_grads",
-    )(table, grads)
+        cost_estimate=pl.CostEstimate(flops=flops, bytes_accessed=4 * q.size * 2, transcendentals=q.size),
+        name="attend_scatter",
+    )(table, cont_len, q, do, ck, cv, pre)
+
+
+def finish_kernel(per, named_ref, out_ref, dq_ref, tail_ref, k_ref, v_ref, out, dq, dk, dv, gk, gv, ob, dqb, tb, kb, vb, first, last):
+    slots = out.shape[0]
+    nz = out_ref.shape[0] // NY
+    dp = lax.axis_index("dp")
+    z, y = dp // NY, dp % NY
+    copy = pltpu.make_async_copy
+    moved = ((k_ref, kb, gk), (v_ref, vb, gv))
+
+    def fetch(s, w):
+        pairs = ((out_ref, ob), (dq_ref, dqb), (tail_ref, tb))
+        return [copy(src.at[w], dst.at[s], first.at[i, s]) for i, (src, dst) in enumerate(pairs)]
+
+    def store(s):
+        pairs = ((ob, out), (dqb, dq))
+        return [copy(src.at[s], dst.at[s], last.at[i, s]) for i, (src, dst) in enumerate(pairs)]
+
+    def begin(s, carry):
+        owner = lax.div(named_ref[dp * slots + s], per)
+        row = lax.rem(z - owner // NY + nz, nz)
+        for c in fetch(s, row * NY + lax.rem(y - owner % NY + NY, NY)):
+            c.start()
+        return carry
+
+    def pass_on(s, carry):
+        for c in fetch(s, 0):
+            c.wait()
+        for c in store(s):
+            c.start()
+        return carry
+
+    def end(s, carry):
+        for c in store(s):
+            c.wait()
+        return carry
+
+    lax.fori_loop(0, slots, begin, 0)
+    for i, (src, buf, _) in enumerate(moved):
+        copy(src, buf, first.at[3, i]).start()
+    lax.fori_loop(0, slots, pass_on, 0)
+    ends = [copy(tb.at[:, i], dst, last.at[2, i]) for i, dst in enumerate((dk, dv))]
+    for i, (src, buf, dst) in enumerate(moved):
+        copy(src, buf, first.at[3, i]).wait()
+        ends.append(copy(buf, dst, last.at[3, i]))
+    for c in ends:
+        c.start()
+    lax.fori_loop(0, slots, end, 0)
+    for c in ends:
+        c.wait()
+
+
+def finish(per, slots, named, out, dq, tail, gk, gv):
+    shape = jax.ShapeDtypeStruct
+    anywhere = pl.BlockSpec(memory_space=pl.ANY)
+    wide = shape((slots,) + out.shape[1:], BF16)
+    thin = shape((slots,) + tail.shape[2:], BF16)
+    dma = pltpu.SemaphoreType.DMA
+    return pl.pallas_call(
+        functools.partial(finish_kernel, per),
+        out_shape=(wide, wide, thin, thin, shape(gk.shape, F32), shape(gv.shape, F32)),
+        in_specs=[pl.BlockSpec(memory_space=pltpu.SMEM)] + [anywhere] * 5,
+        out_specs=[anywhere] * 6,
+        scratch_shapes=[
+            pltpu.VMEM(wide.shape, BF16),
+            pltpu.VMEM(wide.shape, BF16),
+            pltpu.VMEM((slots,) + tail.shape[1:], BF16),
+            pltpu.VMEM(gk.shape, F32),
+            pltpu.VMEM(gv.shape, F32),
+            dma((4, slots)),
+            dma((4, slots)),
+        ],
+        compiler_params=pltpu.CompilerParams(vmem_limit_bytes=FINISH_LIMIT),
+        name="finish",
+    )(named, out, dq, tail, gk, gv)
 
 
 def dot(a, b, dims):
@@ -349,69 +525,13 @@
     probs = exponent * (1.0 / jnp.sum(exponent, axis=0, keepdims=True))
     weights = probs.astype(BF16)
     delta = jnp.sum(probs * dweights, axis=0, keepdims=True)
-    dscores = (probs * (dweights - delta) * scale).astype(BF16)
-    out = dot(weights, values, ((0,), (0,)))
-    out = jnp.where(valid, out, 0.0).astype(BF16)
-    dq = dot(dscores, keys, ((0,), (0,))).astype(BF16)
-    dk = dot(dscores, queries, ((1,), (0,)))
-    dv = dot(weights, cotangent, ((1,), (0,)))
+    dscores = (probs * ((dweights - delta) * scale)).astype(BF16)
+    out = dot(values, weights, ((0,), (0,))).astype(BF16).T
+    out = jnp.where(valid, out, jnp.zeros_like(out))
+    dq = dot(keys, dscores, ((0,), (0,))).astype(BF16).T
+    dk = dot(dscores, queries, ((1,), (0,))).astype(BF16)
+    dv = dot(weights, cotangent, ((1,), (0,))).astype(BF16)
     return out, dq, dk, dv
-
-
-def attend_kernel(
-    batch, per, named_ref, len_ref, q_ref, do_ref, ck_ref, cv_ref, pre_ref, out_ref, dq_ref, dk_ref, dv_ref, g_ref
-):
-    step = pl.program_id(0)
-    dp = lax.axis_index("dp")
-    slots = len_ref.shape[0]
-    nz = pre_ref.shape[0] // NY
-    heads = q_ref.shape[2] // HD
-    tokens = q_ref.shape[1]
-    prefix = pre_ref.shape[2]
-    for b in range(batch):
-        s = step * batch + b
-        owner = named_ref[dp * slots + s] // per
-        row = lax.rem(dp // NY - owner // NY + nz, nz)
-        place = row * NY + lax.rem(dp % NY - owner % NY + NY, NY)
-        queries = jnp.concatenate([q_ref[b, :, h * HD : (h + 1) * HD] for h in range(heads)], axis=0)
-        cotangent = jnp.concatenate([do_ref[b, :, h * HD : (h + 1) * HD] for h in range(heads)], axis=0)
-        keys = jnp.concatenate([pre_ref[place, 0], ck_ref[b]], axis=0)
-        values = jnp.concatenate([pre_ref[place, 1], cv_ref[b]], axis=0)
-        out, dq, dk, dv = attend_slot(len_ref[s], queries, cotangent, keys, values, heads)
-        for h in range(heads):
-            out_ref[b, :, h * HD : (h + 1) * HD] = out[h * tokens : (h + 1) * tokens]
-            dq_ref[b, :, h * HD : (h + 1) * HD] = dq[h * tokens : (h + 1) * tokens]
-        dk_ref[b] = dk[prefix:].astype(BF16)
-        dv_ref[b] = dv[prefix:].astype(BF16)
-        g_ref[place, 0] = dk[:prefix].astype(BF16)
-        g_ref[place, 1] = dv[:prefix].astype(BF16)
-
-
-def attend(per, named, cont_len, q, do, ck, cv, pre, batch=2):
-    slots, tokens, width = q.shape
-    wide = pl.BlockSpec((batch, tokens, width), lambda i, *_: (i, 0, 0))
-    thin = pl.BlockSpec((batch, tokens, HD), lambda i, *_: (i, 0, 0))
-    whole = pl.BlockSpec(pre.shape, lambda i, *_: (0, 0, 0, 0))
-    flops = 12 * slots * tokens * (tokens + pre.shape[2]) * width
-    return pl.pallas_call(
-        functools.partial(attend_kernel, batch, per),
-        grid_spec=pltpu.PrefetchScalarGridSpec(
-            num_scalar_prefetch=2,
-            grid=(slots // batch,),
-            in_specs=[wide, wide, thin, thin, whole],
-            out_specs=[wide, wide, thin, thin, whole],
-        ),
-        out_shape=(
-            jax.ShapeDtypeStruct(q.shape, BF16),
-            jax.ShapeDtypeStruct(q.shape, BF16),
-            jax.ShapeDtypeStruct(ck.shape, BF16),
-            jax.ShapeDtypeStruct(cv.shape, BF16),
-            jax.ShapeDtypeStruct(pre.shape, BF16),
-        ),
-        compiler_params=pltpu.CompilerParams(vmem_limit_bytes=VMEM_LIMIT),
-        cost_estimate=pl.CostEstimate(flops=flops, bytes_accessed=4 * q.size * 2, transcendentals=q.size),
-        name="attend",
-    )(named, cont_len, q, do, ck, cv, pre)
 
 
 def on_device(n_dp, n_t, cont_q, cont_k, cont_v, out_grad, prompt_k, prompt_v, cont_len, cont_prompt):
@@ -419,11 +539,13 @@
     per, share = prompt_k.shape[:2]
     owner = lax.broadcasted_iota(jnp.int32, (1, 1, n_dp), 2)
     offset = cont_prompt.reshape(n_dp, slots, 1) - owner * per
-    table = jnp.max(jnp.where((offset >= 0) & (offset < per), offset, -1), axis=1)
+    slot = lax.broadcasted_iota(jnp.int32, (1, slots, 1), 1)
+    table = jnp.max(jnp.where((offset >= 0) & (offset < per), slot * PACK + offset, -1), axis=1)
     pre = gather_prompts(n_dp, n_t, table, prompt_k, prompt_v)
-    out, dq, dk, dv, grads = attend(per, cont_prompt, cont_len, cont_q, out_grad, cont_k, cont_v, pre)
-    gk, gv = scatter_grads(n_dp, n_t, table, grads, per, share)
-    return out, dq, dk, dv, gk, gv
+    out, dq, tail, gk, gv = attend_scatter(
+        n_dp, n_t, table, cont_len, cont_q, out_grad, cont_k, cont_v, pre, per, share
+    )
+    return finish(per, slots, cont_prompt, out, dq, tail, gk, gv)
 
 
 def solution(mesh):

time: 118 us -> 107 us (0.907)
  Pallas kernels: 112 us -> 104 us
  local copies, waits for them, and re-layouts: 4.3 us -> 0.86 us
    pallas_call x2, Pallas kernels: 61.3 us -> 56.4 us  [the longest x1 48.8 us: attend_scatter(): pl.pallas_call(functools.partial(attend_scatter_kernel, n_dp, n_t), out_s...]
    unnamed x2 -> x0, local copies, waits for them, and re-layouts: 3.44 us -> none
    pallas_call x1, Pallas kernels: 50.9 us -> 47.9 us  [gather_prompts(): pl.pallas_call(functools.partial(gather_kernel, n_dp, n_t), out_shape=jax...]
where the time goes in v3:
time: 107 us
  Pallas kernels  104 us (97%)
    pallas_call x1, Pallas kernels, attend_scatter(): pl.pallas_call(functools.partial(attend_scatter_kernel, n_dp, n_t), out_s...  48.8 us
    pallas_call x1, Pallas kernels, gather_prompts(): pl.pallas_call(functools.partial(gather_kernel, n_dp, n_t), out_shape=jax...  47.9 us
    pallas_call x1, Pallas kernels, finish(): pl.pallas_call(functools.partial(finish_kernel, per), out_shape=(wide, wi...  7.58 us

profile of v3, /device:TPU:1, one launch (start us, length us, event | category | flops | bytes accessed | tf_op | source)
XLA Modules:
  0.0 106.6 jit_solution(12626240650174263320)
XLA Ops:
  0.7 0.8 sub.15
  1.4 0.1 copy.14
  1.5 0.8 fusion.1.m_ref
  2.3 47.9 %gather_prompts.1.pre_ref = bf16[32,2,128,128]{3,2,1,0:T(8,128)(2,1)} custom-call(s32[32,32]{1,0:T(8,128)} %fusion.1.m_ref, bf16[5,16,1024]{2,1,0:T(8,128)(2,1)} %pk_ref.1, bf16[5,16,1024]{2,1,0:T(8,128)(2,1)} %pv_ref.1), custom_call_target="tpu_custom_call" | custom-call | tf_op jit(solution)/shard_map/gather_prompts/pallas_call | solution.py:163
  50.3 48.8 %attend_scatter.1 = (bf16[32,64,1024]{2,1,0:T(8,128)(2,1)}, bf16[32,64,1024]{2,1,0:T(8,128)(2,1)}, bf16[32,2,64,128]{3,2,1,0:T(8,128)(2,1)}, f32[5,16,1024]{2,1,0:T(8,128)}, f32[5,16,1024]{2,1,0:T(8,128)}) custom-call(s32[32,32]{1,0:T(8,128)} %fusion.1.m_ref, s32[20]{0:T(128)} %len_ref.1, bf16[20,64,1024]{2,1,0:T(8,128)(2,1)} %q_ref.1, ...), custom_call_target="tpu_custom_call" | custom-call | flops 4831838208 | bytes 10485760 | tf_op jit(solution)/shard_map/attend_scatter/pallas_call | solution.py:388
  99.0 7.6 %finish.1 = (bf16[20,64,1024]{2,1,0:T(8,128)(2,1)}, bf16[20,64,1024]{2,1,0:T(8,128)(2,1)}, bf16[20,64,128]{2,1,0:T(8,128)(2,1)}, bf16[20,64,128]{2,1,0:T(8,128)(...) custom-call(s32[640]{0:T(1024)} %named_ref.1, bf16[32,64,1024]{2,1,0:T(8,128)(2,1)} %get-tuple-element.11.out_ref, ...), custom_call_target="tpu_custom_call" | custom-call | tf_op jit(solution)/shard_map/finish/pallas_call | solution.py:486
  (2 shorter events, 0.0 us)

commit v4 on v3

--- a/solution.py
+++ b/solution.py
@@ -66,148 +66,30 @@
     )
 
 
-def gather_kernel(n_dp, n_t, m_ref, pk_ref, pv_ref, out_ref, *scratch):
+def fused_kernel(
+    n_dp, n_t, named_ref, len_ref, q_ref, do_ref, ck_ref, cv_ref, pk_ref, pv_ref, out_ref, dq_ref, tail_ref, ok_ref, ov_ref, *scratch
+):
     nz = n_dp // NY
     half = nz // 2
     blocks = [list(scratch[:nz]), list(scratch[nz : 2 * nz])]
-    picked, xs, xr, xl, zs, zr, ys, yr, yl = scratch[2 * nz :]
+    table, picked, qb, dob, ckb, cvb, preb, ob, dqb, tailb, g_ref = scratch[2 * nz : 2 * nz + 11]
+    arrived, far, chain, term, total, pieces = scratch[2 * nz + 11 : 2 * nz + 17]
+    ins, outs, ys, yr, yl, fs, fr, zs, zr, xs, xr, bs, br, bl, hs, hr, ks, kr = scratch[2 * nz + 17 :]
     z, y, t, at_z, at_y, at_t, at_zy = coordinates(n_dp, n_t)
-    share = pk_ref.shape[1]
-    greet(partners(n_t, at_z, at_y, at_t, at_zy))
-    sent = []
-
-    def start(*args):
-        copy = remote(*args)
-        copy.start()
-        sent.append(copy)
-
+    per, share = ok_ref.shape[:2]
+    slots, tokens, width = q_ref.shape
+    heads = width // HD
+    prefix = share * n_t
     mine = pl.ds(pl.multiple_of(t * share, share), share)
     own = pl.ds(pl.multiple_of(t * HD, HD), HD)
-    local = []
-    for kv, ref in enumerate((pk_ref, pv_ref)):
-        for copy in sent:
-            copy.wait_send()
-        sent.clear()
-        for j in range(1, n_t):
-            to = at_t(j)
-            cols = pl.ds(pl.multiple_of(to[1] * HD, HD), HD)
-            start(ref.at[:, :, cols], blocks[kv][0].at[:, mine, :], xs.at[kv, j], xr.at[kv, j], to)
-        local.append(pltpu.make_async_copy(ref.at[:, :, own], blocks[kv][0].at[:, mine, :], xl.at[kv]))
-        local[kv].start()
-
-    def wait_own(kv):
-        local[kv].wait()
-        for j in range(1, n_t):
-            rows = pl.ds(pl.multiple_of(at_t(-j)[1] * share, share), share)
-            remote(
-                (pk_ref, pv_ref)[kv].at[:, :, own], blocks[kv][0].at[:, rows, :], xs.at[kv, j], xr.at[kv, j], at_t(j)
-            ).wait_recv()
-
-    def push(kv, r, way):
-        nxt = (r + way) % nz
-        start(blocks[kv][r], blocks[kv][nxt], zs.at[kv, nxt], zr.at[kv, nxt], at_z(way))
-
-    def wait_block(kv, r):
-        remote(blocks[kv][r], blocks[kv][r], zs.at[kv, r], zr.at[kv, r], at_z(1)).wait_recv()
-
-    def spread(kv, r, way):
-        row = lax.rem(z - r + nz, nz)
-        there = (r + way) % nz
-        for u in (2, 1, 3, 0):
-            to = at_zy(way, u)
-            pick = lax.rem(jnp.maximum(m_ref[to[0], row * NY + y], 0), PACK)
-            picked[there, u, kv] = blocks[kv][r][pick]
-            place = out_ref.at[there * NY + u, kv]
-            if u == 0 and way == 0:
-                copy = pltpu.make_async_copy(picked.at[there, u, kv], place, yl.at[there, kv])
-                copy.start()
-                local.append(copy)
-            else:
-                start(picked.at[there, u, kv], place, ys.at[there, u, kv], yr.at[there, u, kv], to)
-
-    for kv in range(2):
-        wait_own(kv)
-        push(kv, 0, 1)
-        push(kv, 0, -1)
-    for kv in range(2):
-        spread(kv, 0, 0)
-    for h in range(1, half):
-        for kv in range(2):
-            for r, way in ((h, 1), (nz - h, -1)):
-                wait_block(kv, r)
-                if h < half - 1:
-                    push(kv, r, way)
-                elif kv == (0 if way == 1 else 1):
-                    spread(kv, r, way)
-            for r in (h, nz - h):
-                spread(kv, r, 0)
-    for copy in local[2:]:
-        copy.wait()
-    for copy in sent:
-        copy.wait_send()
-    for r in range(nz):
-        for u in range(NY):
-            for kv in range(2):
-                if u or r == half:
-                    place = out_ref.at[r * NY + u, kv]
-                    remote(
-                        picked.at[r, u, kv], place, ys.at[r, u, kv], yr.at[r, u, kv], at_y(1)
-                    ).wait_recv()
-
-
-def gather_prompts(n_dp, n_t, table, pk, pv, cid=0):
-    nz = n_dp // NY
-    per, share, width = pk.shape
-    plen = share * n_t
-    dma = pltpu.SemaphoreType.DMA
-    return pl.pallas_call(
-        functools.partial(gather_kernel, n_dp, n_t),
-        out_shape=jax.ShapeDtypeStruct((n_dp, 2, plen, HD), BF16),
-        in_specs=[
-            pl.BlockSpec(memory_space=pltpu.SMEM),
-            pl.BlockSpec(memory_space=pl.ANY),
-            pl.BlockSpec(memory_space=pl.ANY),
-        ],
-        out_specs=pl.BlockSpec(memory_space=pl.ANY),
-        scratch_shapes=[pltpu.VMEM((per, plen, HD), BF16) for _ in range(2 * nz)]
-        + [
-            pltpu.VMEM((nz, NY, 2, plen, HD), BF16),
-            dma((2, n_t)),
-            dma((2, n_t)),
-            dma((2,)),
-            dma((2, nz)),
-            dma((2, nz)),
-            dma((nz, NY, 2)),
-            dma((nz, NY, 2)),
-            dma((nz, 2)),
-        ],
-        compiler_params=pltpu.CompilerParams(
-            collective_id=cid, has_side_effects=True, vmem_limit_bytes=VMEM_LIMIT
-        ),
-        name="gather_prompts",
-    )(table, pk, pv)
-
-
-def attend_scatter_kernel(
-    n_dp, n_t, m_ref, len_ref, q_ref, do_ref, ck_ref, cv_ref, pre_ref, out_ref, dq_ref, tail_ref, ok_ref, ov_ref, *scratch
-):
-    nz = n_dp // NY
-    half = nz // 2
-    qb, dob, ckb, cvb, preb, ob, dqb, tailb, g_ref = scratch[:9]
-    arrived, far, chain, term, total, pieces, ins, pres, outs, ys, yr, yl, fs, fr, zs, zr, xs, xr = scratch[9:]
-    z, y, t, at_z, at_y, at_t, at_zy = coordinates(n_dp, n_t)
-    per, share = ok_ref.shape[:2]
-    dp = z * NY + y
-    slots, tokens, width = q_ref.shape
-    heads = width // HD
-    prefix = pre_ref.shape[2]
     local = [
         pltpu.make_async_copy(src, dst, ins.at[i])
         for i, (src, dst) in enumerate(((q_ref, qb), (do_ref, dob), (ck_ref, ckb), (cv_ref, cvb)))
     ]
-
-    def prompts(r):
-        return pltpu.make_async_copy(pre_ref.at[pl.ds(r * NY, NY)], preb.at[pl.ds(r * NY, NY)], pres.at[r])
+    owned = [
+        pltpu.make_async_copy(ref.at[:, :, own], blocks[kv][0].at[:, mine, :], bl.at[kv])
+        for kv, ref in enumerate((pk_ref, pv_ref))
+    ]
 
     def results(r):
         part = pl.ds(r * NY, NY)
@@ -216,15 +98,69 @@
             for i, (src, dst) in enumerate(((ob, out_ref), (dqb, dq_ref), (tailb, tail_ref)))
         ]
 
-    for copy in local:
-        copy.start()
-    order = [half]
-    for h in range(half - 1, 0, -1):
-        order += [h, nz - h]
-    order.append(0)
-    for r in order:
-        prompts(r).start()
-    greet(partners(n_t, at_z, at_y, at_t, at_zy))
+    def share_copy(kv, j):
+        to = at_t(j)
+        cols = pl.ds(pl.multiple_of(to[1] * HD, HD), HD)
+        src = (pk_ref, pv_ref)[kv].at[:, :, cols]
+        return remote(src, blocks[kv][0].at[:, mine, :], bs.at[kv, j], br.at[kv, j], to)
+
+    def wait_own(kv):
+        owned[kv].wait()
+        for j in range(1, n_t):
+            rows = pl.ds(pl.multiple_of(at_t(-j)[1] * share, share), share)
+            src = (pk_ref, pv_ref)[kv].at[:, :, own]
+            remote(src, blocks[kv][0].at[:, rows, :], bs.at[kv, j], br.at[kv, j], at_t(j)).wait_recv()
+
+    def block_copy(kv, r, way):
+        nxt = (r + way) % nz
+        return remote(blocks[kv][r], blocks[kv][nxt], hs.at[kv, nxt], hr.at[kv, nxt], at_z(way))
+
+    def wait_block(kv, r):
+        remote(blocks[kv][r], blocks[kv][r], hs.at[kv, r], hr.at[kv, r], at_z(1)).wait_recv()
+
+    def pick_copy(kv, r, u, way=0):
+        place = preb.at[r * NY + u, kv]
+        return remote(picked.at[r, u, kv], place, ks.at[r, u, kv], kr.at[r, u, kv], at_zy(way, u))
+
+    def spread(kv, r, way=0):
+        there = (r + way) % nz
+        for u in (2, 1, 3, 0):
+            name = table[2, kv * NY + u] if way else table[0, r * NY + u]
+            pick = lax.rem(jnp.maximum(name, 0), PACK)
+            if u == 0 and way == 0:
+                preb[r * NY, kv] = blocks[kv][r][pick]
+            else:
+                picked[there, u, kv] = blocks[kv][r][pick]
+                pick_copy(kv, there, u, way).start()
+
+    def gather(kv, h):
+        if h == 0:
+            wait_own(kv)
+            block_copy(kv, 0, 1).start()
+            block_copy(kv, 0, -1).start()
+            return
+        for r, way in ((h, 1), (nz - h, -1)):
+            wait_block(kv, r)
+            if h < half - 1:
+                block_copy(kv, r, way).start()
+            elif kv == (0 if way == 1 else 1):
+                spread(kv, r, way)
+        for r in (h, nz - h):
+            spread(kv, r)
+
+    def entry(device, owner):
+        found = jnp.int32(-1)
+        for s in range(slots):
+            offset = named_ref[device * slots + s] - owner * per
+            found = jnp.where((offset >= 0) & (offset < per), s * PACK + offset, found)
+        return found
+
+    def fill(r, carry):
+        row = lax.rem(z - r + nz, nz) * NY
+        for u in range(NY):
+            table[0, r * NY + u] = entry(at_y(u)[0], row + y)
+            table[1, r * NY + u] = entry(z * NY + y, row + at_y(-u)[0] - z * NY)
+        return carry
 
     def far_copy(kv, u):
         src = g_ref.at[half * NY + u, kv]
@@ -259,12 +195,9 @@
             out_copy(kv, r, u).wait_recv()
 
     def sums(kv, r, store):
-        row = lax.rem(z - r + nz, nz)
-        column = row * NY + y
-        parts = [(lax.rem(m_ref[at_y(u)[0], column], PACK), arrived.at[r, u, kv]) for u in range(NY)]
+        parts = [(lax.rem(table[0, r * NY + u], PACK), arrived.at[r, u, kv]) for u in range(NY)]
         if r == (half - 1 if kv == 0 else half + 1):
-            way = 1 if kv == 0 else -1
-            parts += [(lax.rem(m_ref[at_zy(way, u)[0], column], PACK), far.at[kv, u]) for u in range(NY)]
+            parts += [(lax.rem(table[2, kv * NY + u], PACK), far.at[kv, u]) for u in range(NY)]
         for p in range(per):
             acc = None
             for which, ref in parts:
@@ -289,11 +222,12 @@
         chain_copy(kv, r).start()
 
     def compute(r):
-        row = lax.rem(z - r + nz, nz)
-        prompts(r).wait()
+        for u in range(1, NY):
+            for kv in range(2):
+                pick_copy(kv, r, u).wait_recv()
         for u in range(NY):
             w = r * NY + u
-            slot = lax.div(jnp.maximum(m_ref[dp, row * NY + lax.rem(y - u + NY, NY)], 0), PACK)
+            slot = lax.div(jnp.maximum(table[1, w], 0), PACK)
             queries = jnp.concatenate([qb[slot, :, h * HD : (h + 1) * HD] for h in range(heads)], axis=0)
             cotangent = jnp.concatenate([dob[slot, :, h * HD : (h + 1) * HD] for h in range(heads)], axis=0)
             keys = jnp.concatenate([preb[w, 0], ckb[slot]], axis=0)
@@ -319,31 +253,67 @@
             for r in (h, nz - h):
                 reduce_block(kv, r)
 
+    for copy in local:
+        copy.start()
+    for copy in owned:
+        copy.start()
+    greet(partners(n_t, at_z, at_y, at_t, at_zy))
+    for kv in range(2):
+        for j in range(1, n_t):
+            share_copy(kv, j).start()
+    lax.fori_loop(0, nz, fill, 0)
+    for kv, way in enumerate((1, -1)):
+        row = lax.rem(z - way * (half - 1) + nz, nz)
+        for u in range(NY):
+            table[2, kv * NY + u] = entry(at_zy(way, u)[0], row * NY + y)
+    gather(0, 0)
+    gather(1, 0)
+    for kv in range(2):
+        spread(kv, 0)
+    gather(0, 1)
+    gather(1, 1)
+    for copy in local:
+        copy.wait()
+
+    def ahead(i):
+        if i in (1, 2, 3, 4):
+            gather((i + 1) % 2, (i + 3) // 2)
+        elif i == nz - 1:
+            for kv in range(2):
+                pick_copy(kv, half, 0).wait_recv()
+
     def after(i):
-        if i == 0:
+        if i == 4:
+            for kv in range(2):
+                send_out(kv, 2)
+        elif i in (5, 6):
+            for kv in range(2):
+                send_out(kv, 3 if i == 5 else 5)
+        elif i == nz - 1:
             for kv in range(2):
                 for u in range(NY):
                     far_copy(kv, u).start()
-            return
-        for kv in range(2):
-            send_out(kv, order[i])
-        if i >= 4 and i % 2 == 0:
-            hop(half + 1 - i // 2)
 
     def step(i, carry):
-        back = lax.div(i + 1, 2)
-        sign = 2 * lax.rem(i + 1, 2) - 1
-        compute(lax.rem(half + sign * back + nz, nz))
-        for j in range(nz):
+        for j in (1, 2, 3, 4, nz - 1):
+            pl.when(i == j)(functools.partial(ahead, j))
+        sign = 2 * lax.rem(i, 2) - 1
+        compute(lax.rem(sign * lax.div(i + 1, 2) + nz, nz))
+        for j in (4, 5, 6, nz - 1):
             pl.when(i == j)(functools.partial(after, j))
         return carry
 
-    for copy in local:
-        copy.wait()
     lax.fori_loop(0, nz, step, 0)
+    for kv in range(2):
+        send_out(kv, 6)
+    hop(3)
+    for kv in range(2):
+        for r in (1, 7):
+            send_out(kv, r)
+    hop(2)
+    for kv in range(2):
+        send_out(kv, 0)
     hop(1)
-    mine = pl.ds(pl.multiple_of(t * share, share), share)
-    own = pl.ds(pl.multiple_of(t * HD, HD), HD)
     for kv in range(2):
         wait_y(kv, 0)
         sums(kv, 0, term.at[0])
@@ -359,24 +329,33 @@
             cols = pl.ds(pl.multiple_of(at_t(-j)[1] * HD, HD), HD)
             (ok_ref, ov_ref)[kv][:, :, cols] = pieces[kv, j].astype(F32)
     for kv in range(2):
+        for j in range(1, n_t):
+            share_copy(kv, j).wait_send()
+            piece_copy(kv, j).wait_send()
         for u in range(NY):
             far_copy(kv, u).wait_send()
-        for r in order[1:]:
+            pick_copy(kv, half, u, 1 if kv == 0 else -1).wait_send()
+        for r in range(nz):
+            if r == half:
+                continue
             for u in range(1, NY):
+                pick_copy(kv, r, u).wait_send()
                 out_copy(kv, r, u).wait_send()
             if r:
                 chain_copy(kv, r).wait_send()
-        for j in range(1, n_t):
-            piece_copy(kv, j).wait_send()
+        for r in range(half - 1):
+            block_copy(kv, r, 1).wait_send()
+            block_copy(kv, (nz - r) % nz, -1).wait_send()
     for r in range(nz):
         for copy in results(r):
             copy.wait()
 
 
-def attend_scatter(n_dp, n_t, table, cont_len, q, do, ck, cv, pre, per, share, cid=1):
+def fused(n_dp, n_t, named, cont_len, q, do, ck, cv, pk, pv):
     nz = n_dp // NY
     slots, tokens, width = q.shape
-    plen = pre.shape[2]
+    per, share = pk.shape[:2]
+    plen = share * n_t
     dma = pltpu.SemaphoreType.DMA
     shape = jax.ShapeDtypeStruct
     anywhere = pl.BlockSpec(memory_space=pl.ANY)
@@ -384,30 +363,33 @@
     part = shape((per, share, n_t * HD), F32)
     wide = (n_dp, tokens, width)
     tails = (n_dp, 2, tokens, HD)
+    pairs = (nz, NY, 2, plen, HD)
     flops = 12 * n_dp * tokens * (tokens + plen) * width
     return pl.pallas_call(
-        functools.partial(attend_scatter_kernel, n_dp, n_t),
+        functools.partial(fused_kernel, n_dp, n_t),
         out_shape=(shape(wide, BF16), shape(wide, BF16), shape(tails, BF16), part, part),
-        in_specs=[scalars, scalars] + [anywhere] * 5,
+        in_specs=[scalars, scalars] + [anywhere] * 6,
         out_specs=[anywhere] * 3 + [pl.BlockSpec(memory_space=pltpu.VMEM)] * 2,
-        scratch_shapes=[
+        scratch_shapes=[pltpu.VMEM((per, plen, HD), BF16) for _ in range(2 * nz)]
+        + [
+            pltpu.SMEM((3, n_dp), jnp.int32),
+            pltpu.VMEM(pairs, BF16),
             pltpu.VMEM(q.shape, BF16),
             pltpu.VMEM(q.shape, BF16),
             pltpu.VMEM(ck.shape, BF16),
             pltpu.VMEM(ck.shape, BF16),
-            pltpu.VMEM(pre.shape, BF16),
+            pltpu.VMEM((n_dp, 2, plen, HD), BF16),
             pltpu.VMEM(wide, BF16),
             pltpu.VMEM(wide, BF16),
             pltpu.VMEM(tails, BF16),
-            pltpu.VMEM(pre.shape, BF16),
-            pltpu.VMEM((nz, NY, 2, plen, HD), BF16),
+            pltpu.VMEM((n_dp, 2, plen, HD), BF16),
+            pltpu.VMEM(pairs, BF16),
             pltpu.VMEM((2, NY, plen, HD), BF16),
             pltpu.VMEM((2, 2, nz, per, plen, HD), BF16),
             pltpu.VMEM((2, per, plen, HD), F32),
             pltpu.VMEM((2, per, plen, HD), BF16),
             pltpu.VMEM((2, n_t, per, share, HD), BF16),
             dma((4,)),
-            dma((nz,)),
             dma((3, nz)),
             dma((nz, NY, 2)),
             dma((nz, NY, 2)),
@@ -418,13 +400,20 @@
             dma((2, 2, nz)),
             dma((2, n_t)),
             dma((2, n_t)),
+            dma((2, n_t)),
+            dma((2, n_t)),
+            dma((2,)),
+            dma((2, nz)),
+            dma((2, nz)),
+            dma((nz, NY, 2)),
+            dma((nz, NY, 2)),
         ],
         compiler_params=pltpu.CompilerParams(
-            collective_id=cid, has_side_effects=True, vmem_limit_bytes=VMEM_LIMIT
+            collective_id=0, has_side_effects=True, vmem_limit_bytes=VMEM_LIMIT
         ),
         cost_estimate=pl.CostEstimate(flops=flops, bytes_accessed=4 * q.size * 2, transcendentals=q.size),
-        name="attend_scatter",
-    )(table, cont_len, q, do, ck, cv, pre)
+        name="fused",
+    )(named, cont_len, q, do, ck, cv, pk, pv)
 
 
 def finish_kernel(per, named_ref, out_ref, dq_ref, tail_ref, k_ref, v_ref, out, dq, dk, dv, gk, gv, ob, dqb, tb, kb, vb, first, last):
@@ -535,17 +524,10 @@
 
 
 def on_device(n_dp, n_t, cont_q, cont_k, cont_v, out_grad, prompt_k, prompt_v, cont_len, cont_prompt):
-    slots = cont_q.shape[0]
-    per, share = prompt_k.shape[:2]
-    owner = lax.broadcasted_iota(jnp.int32, (1, 1, n_dp), 2)
-    offset = cont_prompt.reshape(n_dp, slots, 1) - owner * per
-    slot = lax.broadcasted_iota(jnp.int32, (1, slots, 1), 1)
-    table = jnp.max(jnp.where((offset >= 0) & (offset < per), slot * PACK + offset, -1), axis=1)
-    pre = gather_prompts(n_dp, n_t, table, prompt_k, prompt_v)
-    out, dq, tail, gk, gv = attend_scatter(
-        n_dp, n_t, table, cont_len, cont_q, out_grad, cont_k, cont_v, pre, per, share
+    out, dq, tail, gk, gv = fused(
+        n_dp, n_t, cont_prompt, cont_len, cont_q, out_grad, cont_k, cont_v, prompt_k, prompt_v
     )
-    return finish(per, slots, cont_prompt, out, dq, tail, gk, gv)
+    return finish(prompt_k.shape[0], cont_q.shape[0], cont_prompt, out, dq, tail, gk, gv)
 
 
 def solution(mesh):

time: 107 us -> 99.2 us (0.927)
  Pallas kernels: 104 us -> 98.4 us
    pallas_call x2 -> x1, Pallas kernels: 96.7 us -> 90.8 us  [fused(): pl.pallas_call(functools.partial(fused_kernel, n_dp, n_t), out_shape=(sha...]
where the time goes in v4:
time: 99.2 us; the launch traced here: 99 us
  Pallas kernels  98.4 us (99%)
    pallas_call x1, Pallas kernels, fused(): pl.pallas_call(functools.partial(fused_kernel, n_dp, n_t), out_shape=(sha...  90.8 us
    pallas_call x1, Pallas kernels, finish(): pl.pallas_call(functools.partial(finish_kernel, per), out_shape=(wide, wi...  7.58 us

profile of v4, /device:TPU:1, one launch (start us, length us, event | category | flops | bytes accessed | tf_op | source)
XLA Modules:
  0.0 99.0 jit_solution(5325999033684850446)
XLA Ops:
  0.6 90.8 %fused.1 = (bf16[32,64,1024]{2,1,0:T(8,128)(2,1)}, bf16[32,64,1024]{2,1,0:T(8,128)(2,1)}, bf16[32,2,64,128]{3,2,1,0:T(8,128)(2,1)}, f32[5,16,1024]{2,1,0:T(8,128)}, f32[5,16,1024]{2,1,0:T(8,128)}) custom-call(s32[640]{0:T(1024)} %named_ref.3, s32[20]{0:T(128)} %len_ref.1, bf16[20,64,1024]{2,1,0:T(8,128)(2,1)} %q_ref.1, bf16[20,64,1024]{2,1,0:T(8,128)(2,1)} %do_ref.1, ...), custom_call_target="tpu_custom_call" | custom-call | flops 4831838208 | bytes 10485760 | tf_op jit(solution)/shard_map/fused/pallas_call | solution.py:368
  91.5 7.6 %finish.1 = (bf16[20,64,1024]{2,1,0:T(8,128)(2,1)}, bf16[20,64,1024]{2,1,0:T(8,128)(2,1)}, bf16[20,64,128]{2,1,0:T(8,128)(2,1)}, bf16[20,64,128]{2,1,0:T(8,128)(...) custom-call(s32[640]{0:T(1024)} %named_ref.3, bf16[32,64,1024]{2,1,0:T(8,128)(2,1)} %get-tuple-element.11.out_ref, ...), custom_call_target="tpu_custom_call" | custom-call | tf_op jit(solution)/shard_map/finish/pallas_call | solution.py:475

commit v5 on v4

--- a/solution.py
+++ b/solution.py
@@ -244,17 +244,13 @@
             copy.start()
 
     def hop(h):
-        for kv in range(2):
-            for r in (h, nz - h):
-                wait_y(kv, r)
-            if h == half - 1:
+        for kv, r in ((1, h), (0, nz - h), (0, h), (1, nz - h)):
+            wait_y(kv, r)
+            if h == half - 1 and kv == (0 if r == h else 1):
                 for u in range(NY):
                     far_copy(kv, u).wait_recv()
-            for r in (h, nz - h):
-                reduce_block(kv, r)
-
-    for copy in local:
-        copy.start()
+            reduce_block(kv, r)
+
     for copy in owned:
         copy.start()
     greet(partners(n_t, at_z, at_y, at_t, at_zy))
@@ -270,36 +266,42 @@
     gather(1, 0)
     for kv in range(2):
         spread(kv, 0)
+    for copy in local:
+        copy.start()
     gather(0, 1)
     gather(1, 1)
     for copy in local:
         copy.wait()
 
     def ahead(i):
-        if i in (1, 2, 3, 4):
-            gather((i + 1) % 2, (i + 3) // 2)
+        if i in (1, 2):
+            gather(i - 1, 2)
+        elif i == 3:
+            gather(0, 3)
+            gather(1, 3)
         elif i == nz - 1:
             for kv in range(2):
                 pick_copy(kv, half, 0).wait_recv()
 
     def after(i):
-        if i == 4:
-            for kv in range(2):
-                send_out(kv, 2)
-        elif i in (5, 6):
-            for kv in range(2):
-                send_out(kv, 3 if i == 5 else 5)
+        if i == 5:
+            send_out(1, 3)
+            send_out(0, 3)
+        elif i == 6:
+            for r in (5, 2):
+                for kv in range(2):
+                    send_out(kv, r)
         elif i == nz - 1:
             for kv in range(2):
                 for u in range(NY):
                     far_copy(kv, u).start()
 
     def step(i, carry):
-        for j in (1, 2, 3, 4, nz - 1):
+        for j in (1, 2, 3, nz - 1):
             pl.when(i == j)(functools.partial(ahead, j))
         sign = 2 * lax.rem(i, 2) - 1
         compute(lax.rem(sign * lax.div(i + 1, 2) + nz, nz))
-        for j in (4, 5, 6, nz - 1):
+        for j in (5, 6, nz - 1):
             pl.when(i == j)(functools.partial(after, j))
         return carry
 
@@ -313,7 +315,29 @@
     hop(2)
     for kv in range(2):
         send_out(kv, 0)
+    for kv in range(2):
+        for j in range(1, n_t):
+            share_copy(kv, j).wait_send()
+        for u in range(NY):
+            far_copy(kv, u).wait_send()
+            pick_copy(kv, half, u, 1 if kv == 0 else -1).wait_send()
+        for r in range(nz):
+            if r == half:
+                continue
+            for u in range(1, NY):
+                pick_copy(kv, r, u).wait_send()
+                if r:
+                    out_copy(kv, r, u).wait_send()
+        for r in range(half - 1):
+            block_copy(kv, r, 1).wait_send()
+            block_copy(kv, (nz - r) % nz, -1).wait_send()
+    for r in range(nz):
+        for copy in results(r):
+            copy.wait()
     hop(1)
+    for kv in range(2):
+        for u in range(1, NY):
+            out_copy(kv, 0, u).wait_send()
     for kv in range(2):
         wait_y(kv, 0)
         sums(kv, 0, term.at[0])
@@ -330,25 +354,9 @@
             (ok_ref, ov_ref)[kv][:, :, cols] = pieces[kv, j].astype(F32)
     for kv in range(2):
         for j in range(1, n_t):
-            share_copy(kv, j).wait_send()
             piece_copy(kv, j).wait_send()
-        for u in range(NY):
-            far_copy(kv, u).wait_send()
-            pick_copy(kv, half, u, 1 if kv == 0 else -1).wait_send()
-        for r in range(nz):
-            if r == half:
-                continue
-            for u in range(1, NY):
-                pick_copy(kv, r, u).wait_send()
-                out_copy(kv, r, u).wait_send()
-            if r:
-                chain_copy(kv, r).wait_send()
-        for r in range(half - 1):
-            block_copy(kv, r, 1).wait_send()
-            block_copy(kv, (nz - r) % nz, -1).wait_send()
-    for r in range(nz):
-        for copy in results(r):
-            copy.wait()
+        for r in (h for h in range(1, nz) if h != half):
+            chain_copy(kv, r).wait_send()
 
 
 def fused(n_dp, n_t, named, cont_len, q, do, ck, cv, pk, pv):

time: 99.2 us -> 97.2 us (0.980)
  Pallas kernels: 98.4 us -> 96.4 us
    pallas_call x1, Pallas kernels: 90.8 us -> 88.8 us  [fused(): pl.pallas_call(functools.partial(fused_kernel, n_dp, n_t), out_shape=(sha...]
where the time goes in v5:
time: 97.2 us; the launch traced here: 97 us
  Pallas kernels  96.4 us (99%)
    pallas_call x1, Pallas kernels, fused(): pl.pallas_call(functools.partial(fused_kernel, n_dp, n_t), out_shape=(sha...  88.8 us
    pallas_call x1, Pallas kernels, finish(): pl.pallas_call(functools.partial(finish_kernel, per), out_shape=(wide, wi...  7.58 us

profile of v5, /device:TPU:1, one launch (start us, length us, event | category | flops | bytes accessed | tf_op | source)
XLA Modules:
  0.0 97.0 jit_solution(16808072105800974544)
XLA Ops:
  0.6 88.8 %fused.1 = (bf16[32,64,1024]{2,1,0:T(8,128)(2,1)}, bf16[32,64,1024]{2,1,0:T(8,128)(2,1)}, bf16[32,2,64,128]{3,2,1,0:T(8,128)(2,1)}, f32[5,16,1024]{2,1,0:T(8,128)}, f32[5,16,1024]{2,1,0:T(8,128)}) custom-call(s32[640]{0:T(1024)} %named_ref.3, s32[20]{0:T(128)} %len_ref.1, bf16[20,64,1024]{2,1,0:T(8,128)(2,1)} %q_ref.1, bf16[20,64,1024]{2,1,0:T(8,128)(2,1)} %do_ref.1, ...), custom_call_target="tpu_custom_call" | custom-call | flops 4831838208 | bytes 10485760 | tf_op jit(solution)/shard_map/fused/pallas_call | solution.py:376
  89.4 7.6 %finish.1 = (bf16[20,64,1024]{2,1,0:T(8,128)(2,1)}, bf16[20,64,1024]{2,1,0:T(8,128)(2,1)}, bf16[20,64,128]{2,1,0:T(8,128)(2,1)}, bf16[20,64,128]{2,1,0:T(8,128)(...) custom-call(s32[640]{0:T(1024)} %named_ref.3, bf16[32,64,1024]{2,1,0:T(8,128)(2,1)} %get-tuple-element.11.out_ref, ...), custom_call_target="tpu_custom_call" | custom-call | tf_op jit(solution)/shard_map/finish/pallas_call | solution.py:483

commit v6 on v5

--- a/solution.py
+++ b/solution.py
@@ -143,10 +143,10 @@
             wait_block(kv, r)
             if h < half - 1:
                 block_copy(kv, r, way).start()
-            elif kv == (0 if way == 1 else 1):
-                spread(kv, r, way)
         for r in (h, nz - h):
             spread(kv, r)
+        if h == half - 1:
+            spread(kv, h if kv == 0 else nz - h, 1 if kv == 0 else -1)
 
     def entry(device, owner):
         found = jnp.int32(-1)

time: 97.2 us -> 96.9 us (level)
  no operation moved by 1% of the time
where the time goes in v6:
time: 96.9 us; the launch traced here: 96.8 us
  Pallas kernels  96.1 us (99%)
    pallas_call x1, Pallas kernels, fused(): pl.pallas_call(functools.partial(fused_kernel, n_dp, n_t), out_shape=(sha...  88.5 us
    pallas_call x1, Pallas kernels, finish(): pl.pallas_call(functools.partial(finish_kernel, per), out_shape=(wide, wi...  7.58 us

profile of v6, /device:TPU:1, one launch (start us, length us, event | category | flops | bytes accessed | tf_op | source)
XLA Modules:
  0.0 96.8 jit_solution(1632823961143013269)
XLA Ops:
  0.6 88.5 %fused.1 = (bf16[32,64,1024]{2,1,0:T(8,128)(2,1)}, bf16[32,64,1024]{2,1,0:T(8,128)(2,1)}, bf16[32,2,64,128]{3,2,1,0:T(8,128)(2,1)}, f32[5,16,1024]{2,1,0:T(8,128)}, f32[5,16,1024]{2,1,0:T(8,128)}) custom-call(s32[640]{0:T(1024)} %named_ref.3, s32[20]{0:T(128)} %len_ref.1, bf16[20,64,1024]{2,1,0:T(8,128)(2,1)} %q_ref.1, bf16[20,64,1024]{2,1,0:T(8,128)(2,1)} %do_ref.1, ...), custom_call_target="tpu_custom_call" | custom-call | flops 4831838208 | bytes 10485760 | tf_op jit(solution)/shard_map/fused/pallas_call | solution.py:376
  89.2 7.6 %finish.1 = (bf16[20,64,1024]{2,1,0:T(8,128)(2,1)}, bf16[20,64,1024]{2,1,0:T(8,128)(2,1)}, bf16[20,64,128]{2,1,0:T(8,128)(2,1)}, bf16[20,64,128]{2,1,0:T(8,128)(...) custom-call(s32[640]{0:T(1024)} %named_ref.3, bf16[32,64,1024]{2,1,0:T(8,128)(2,1)} %get-tuple-element.11.out_ref, ...), custom_call_target="tpu_custom_call" | custom-call | tf_op jit(solution)/shard_map/finish/pallas_call | solution.py:483
